TPU v7x, 256 devices: a whole 4x4x8 slice. The times are simulated.
256 devices in a mesh: gx: 8 (over y, core), gy: 16 (over x_lo, z), gz: 2 (over x_hi).
Axes of the slice: x: 4 (x_hi: 2, x_lo: 2; x = x_hi * 2 + x_lo), y: 4, z: 8, core: 2. Of those that a mesh axis runs over, the one named last changes fastest.
Arguments:
- field: float32 [16, 64, 8, 128], P('gx', 'gy', 'gz'), may hold values from -6 to 6
- parity_mask: int32 [16, 64, 8, 128], P('gx', 'gy', 'gz'), may hold values 0 or 1
- kernel_one: bfloat16 [16, 1, 3, 3, 3, 3], replicated, may hold values from -0.625 to 0.625
- bias_one: float32 [16], replicated, may hold values from -3 to 3
- kernel_two: bfloat16 [16, 16, 3, 3, 3, 3], replicated, may hold values from -0.15625 to 0.15625
- bias_two: float32 [16], replicated, may hold values from -3 to 3
- kernel_three: bfloat16 [2, 16, 3, 3, 3, 3], replicated, may hold values from -0.15625 to 0.15625
- bias_three: float32 [2], replicated, may hold values from -3 to 3
Outputs:
- flowed: float32 [16, 64, 8, 128], P('gx', 'gy', 'gz')
- field_grad: float32 [16, 64, 8, 128], P('gx', 'gy', 'gz')
- grad_kernel_one: float32 [16, 1, 3, 3, 3, 3], replicated
- grad_bias_one: float32 [16], replicated
- grad_kernel_two: float32 [16, 16, 3, 3, 3, 3], replicated
- grad_bias_two: float32 [16], replicated
- grad_kernel_three: float32 [2, 16, 3, 3, 3, 3], replicated
- grad_bias_three: float32 [2], replicated
Inputs may be any that keep to these rules, and one draw needn't show every extreme that they name: parity_mask holds only 0 and 1.
All inputs are finite; a program needn't handle non-finite values. No bound on the sum of `parity_mask` on one device may be relied on, other than what follows from the above.
Results may differ from a plain program's by a relative error of at most 0.0073.
Values may be sent and summed in bfloat16 or wider, within the bound.
No kernel may reach another device: no remote copies, remote signals or barrier semaphores. Data moves between devices by JAX's collectives and lax.ppermute only.
A program may use at most 192 MiB of HBM per device.

v0:
```python
import functools

import jax
import jax.numpy as jnp
import numpy as np
from jax import lax
from jax.experimental import pallas as pl
from jax.experimental.pallas import tpu as pltpu
from jax.sharding import Mesh
from jax.sharding import PartitionSpec as P

F32 = jnp.float32
BF16 = jnp.bfloat16
GROUP = ("gz", "gx", "gyl")
VMEM_SPEC = pl.BlockSpec(memory_space=pltpu.VMEM)
VOLUME = 1048576.0


def lane_permutation():
    matrix = np.zeros((512, 512), np.float32)
    for gz in range(2):
        for gx in range(8):
            for x in range(2):
                for y in range(4):
                    for z in range(4):
                        source = (gz * 8 + gx) * 32 + x * 16 + y * 4 + z
                        target = y * 128 + (15 - gx * 2 - x) * 8 + gz * 4 + z
                        matrix[source, target] = 1.0
    return matrix


def pack_kernel(field_ref, mask_ref, out_ref, window):
    both = jnp.concatenate([field_ref[...], mask_ref[...].astype(F32)], axis=0)
    rolled = jnp.concatenate([pltpu.roll(both, 7, 1), pltpu.roll(both, 119, 1)], axis=0)
    turned = rolled.T
    window[0:128, :] = turned
    window[128:144, :] = turned[0:16, :]
    for slot in range(32):
        out_ref[slot] = window[4 * slot : 4 * slot + 16, :]


def weights_kernel(k2_ref, k2t_ref, k3_ref, k1_ref, w2_ref, w2t_ref, w3_ref, w1t_ref):
    lane = lax.broadcasted_iota(jnp.int32, (16, 128), 1)
    zero = jnp.zeros((16, 128), F32)

    def pick(parts, zone, wanted):
        total = zero
        for part, where in zip(parts, wanted):
            total = jnp.where(zone == where, part, total)
        return total.astype(BF16)

    def body(off, carry):
        k2 = [k2_ref[off * 3 + ez].astype(F32) for ez in range(3)]
        k2t = [k2t_ref[off * 3 + ez].astype(F32) for ez in range(3)]
        k3 = [[k3_ref[off * 3 + ez, o].astype(F32) for ez in range(3)] for o in range(2)]
        k1 = [k1_ref[off * 3 + ez].astype(F32) for ez in range(3)]
        for zin in range(8):
            forward = [(zin - ez + 1) % 8 for ez in range(3)]
            backward = [(zin + ez - 1) % 8 for ez in range(3)]
            rows = pl.ds(pl.multiple_of(off * 128 + zin * 16, 16), 16)
            w2_ref[rows, :] = pick(k2, lane // 16, forward)
            w2t_ref[rows, :] = pick(k2t, lane // 16, backward)
            w3_ref[rows, 0:128] = pick(k3[0], lane % 8, forward)
            w3_ref[rows, 128:256] = pick(k3[1], lane % 8, forward)
            w1t_ref[rows, :] = pick(k1, lane % 8, backward)
        return carry

    lax.fori_loop(0, 27, body, 0)


def split_dot(values, matrix, parts, transposed=False):
    dims = (((1,), (1 if transposed else 0,)), ((), ()))
    total = None
    rest = values
    for _ in range(parts):
        head = rest.astype(BF16)
        rest = rest - head.astype(F32)
        term = lax.dot_general(head, matrix, dims, preferred_element_type=F32)
        total = term if total is None else total + term
    return total


def spread(rows_value, base):
    count = rows_value.shape[0]
    turned = pltpu.roll(rows_value, 16 + base, 1)
    wide = jnp.broadcast_to(turned[:, None, :], (count, 16, 128))
    return pltpu.roll(wide, 0, 2, stride=8, stride_axis=1)


def spread_rows(rows_value):
    count = rows_value.shape[0]
    lane = lax.broadcasted_iota(jnp.int32, (count - 2, 16, 128), 2)
    low = spread(rows_value[0 : count - 2], 0)
    mid = spread(rows_value[1 : count - 1], 24)
    high = spread(rows_value[2:count], 48)
    return jnp.where(lane < 24, low, jnp.where(lane < 48, mid, high))


def store_shifted(ref, time, values):
    ref[time, :, :, 0:128] = pltpu.roll(values, 1, 1).astype(BF16)
    ref[time, :, :, 128:256] = values.astype(BF16)
    ref[time, :, :, 256:384] = pltpu.roll(values, 15, 1).astype(BF16)


def nine_dot(ref, time, rows, w_ref):
    total = None
    for first in range(3):
        for second in range(3):
            block = ref[time + first, second : second + rows].reshape(rows * 16, 384)
            at = (first * 3 + second) * 384
            term = jnp.dot(block, w_ref[at : at + 384, :], preferred_element_type=F32)
            total = term if total is None else total + term
    return total


def diagonal_sum(values, rows):
    lane = 15 - lax.broadcasted_iota(jnp.int32, (rows, 16, 128), 2) // 8
    site = lax.broadcasted_iota(jnp.int32, (rows, 16, 128), 1)
    return jnp.sum(jnp.where(lane == site, values.reshape(rows, 16, 128), 0.0), axis=1)


def fold_group(values):
    lane = lax.broadcasted_iota(jnp.int32, values.shape, 1)
    for step in (1, 2, 4):
        down = pltpu.roll(values, 128 - step, 1)
        up = pltpu.roll(values, step, 1)
        values = values + jnp.where((lane // step) % 2 == 0, down, up)
    return values


def main_kernel(
    low_ref, own_ref, high_ref, perm_ref, w1_ref, w3t_ref, w2_ref, w2t_ref, w3_ref, w1t_ref, bias_ref,
    out_ref,
    gather_f, gather_m, dense_f, dense_m, frozen_x, act1, act2, pre0, pre1, flow, scale_c, shift_c, direct,
    third_x, cot2, cot1, own_out, rows_out,
):
    for block, ref in enumerate((low_ref, own_ref, high_ref)):
        for source in range(32):
            spot, half = source // 2, source % 2
            lanes = slice(spot * 32, spot * 32 + 32)
            piece = ref[source]
            gather_f[block * 2 + half, 0:16, lanes] = piece[:, 0:32]
            gather_m[block * 2 + half, 0:16, lanes] = piece[:, 32:64]
            gather_f[block * 2 + half, 16:24, lanes] = piece[0:8, 64:96]
            gather_m[block * 2 + half, 16:24, lanes] = piece[0:8, 96:128]
    perm = perm_ref[...]
    sorted_f = split_dot(gather_f[...].reshape(144, 512), perm, 3)
    sorted_m = split_dot(gather_m[...].reshape(144, 512), perm, 1)
    for block in range(6):
        for y in range(4):
            lanes = slice(y * 128, y * 128 + 128)
            rows = pl.ds(block * 4 + y, 18, stride=24)
            dense_f[rows, :] = sorted_f[block * 24 : block * 24 + 18, lanes]
            dense_m[rows, :] = sorted_m[block * 24 : block * 24 + 18, lanes]

    def spread_frozen(time, carry):
        rows = pl.ds(pl.multiple_of(time * 24, 8), 24)
        frozen = (dense_f[rows, :] * dense_m[rows, :]).astype(BF16).astype(F32)
        frozen_x[time] = spread_rows(frozen[1:23]).astype(BF16)
        return carry

    lax.fori_loop(0, 18, spread_frozen, 0)

    def first_layer(time, carry):
        total = bias_ref[0:1, :]
        for first in range(3):
            block = frozen_x[time + first].reshape(320, 128)
            total = total + jnp.dot(
                block, w1_ref[first * 128 : first * 128 + 128, :], preferred_element_type=F32
            )
        store_shifted(act1, time, jnp.tanh(total).reshape(20, 16, 128))
        return carry

    lax.fori_loop(0, 16, first_layer, 0)

    def second_layer(time, carry):
        total = nine_dot(act1, time, 18, w2_ref) + bias_ref[1:2, :]
        store_shifted(act2, time, jnp.tanh(total).reshape(18, 16, 128))
        return carry

    lax.fori_loop(0, 14, second_layer, 0)

    def third_layer(time, carry):
        total = nine_dot(act2, time, 16, w3_ref)
        pre0[time] = diagonal_sum(total[:, 0:128], 16) + bias_ref[2:3, :]
        pre1[time] = diagonal_sum(total[:, 128:256], 16) + bias_ref[3:4, :]
        return carry

    lax.fori_loop(0, 12, third_layer, 0)

    def transform(time, carry):
        rows = pl.ds(pl.multiple_of((time + 3) * 24, 8), 24)
        field = dense_f[rows, :][4:20]
        share = dense_m[rows, :][4:20]
        growth = jnp.exp(jnp.tanh(pre0[time]))
        flow[time] = share * field + (1.0 - share) * (field * growth + pre1[time])
        return carry

    lax.fori_loop(0, 12, transform, 0)

    def force_step(time, carry):
        rows = pl.ds(pl.multiple_of((time + 4) * 24, 8), 24)
        field = dense_f[rows, :][5:19]
        share = dense_m[rows, :][5:19]
        here = flow[time + 1]
        lane = lax.broadcasted_iota(jnp.int32, (16, 128), 1) % 8
        around = flow[time] + flow[time + 2] + pltpu.roll(here, 8, 1) + pltpu.roll(here, 120, 1)
        around = around + jnp.where(lane == 0, pltpu.roll(here, 121, 1), pltpu.roll(here, 1, 1))
        around = around + jnp.where(lane == 7, pltpu.roll(here, 7, 1), pltpu.roll(here, 127, 1))
        around = around[1:15] + here[0:14] + here[2:16]
        mid = here[1:15]
        force = -0.5 * around + 1.8 * mid + 0.2 * mid * mid * mid
        scale = jnp.tanh(pre0[time + 1][1:15])
        growth = jnp.exp(scale)
        active = 1.0 - share
        scale_c[time] = (active * (force * field * growth - 1.0) * (1.0 - scale * scale)).astype(BF16).astype(F32)
        shift_c[time] = (active * force).astype(BF16).astype(F32)
        direct[time] = force * (share + active * growth)
        third_x[time, :, :, 0:128] = spread_rows(scale_c[time]).astype(BF16)
        third_x[time, :, :, 128:256] = spread_rows(shift_c[time]).astype(BF16)
        return carry

    lax.fori_loop(0, 10, force_step, 0)

    def second_cot(time, carry):
        total = None
        for first in range(3):
            block = third_x[time + first].reshape(192, 256)
            term = jnp.dot(
                block, w3t_ref[first * 256 : first * 256 + 256, :], preferred_element_type=F32
            )
            total = term if total is None else total + term
        act = act2[time + 3, 3:15, :, 128:256].astype(F32)
        values = total.reshape(12, 16, 128) * (1.0 - act * act)
        store_shifted(cot2, time, values)
        return carry

    lax.fori_loop(0, 8, second_cot, 0)

    def first_cot(time, carry):
        total = nine_dot(cot2, time, 10, w2t_ref)
        act = act1[time + 5, 5:15, :, 128:256].astype(F32)
        values = total.reshape(10, 16, 128) * (1.0 - act * act)
        store_shifted(cot1, time, values)
        return carry

    lax.fori_loop(0, 6, first_cot, 0)

    for time in range(4):
        total = diagonal_sum(nine_dot(cot1, time, 8, w1t_ref), 8)
        own_out[time * 8 : time * 8 + 8, :] = flow[time + 4][4:12]
        own_out[32 + time * 8 : 40 + time * 8, :] = (
            direct[time + 3][3:11] + dense_m[(time + 7) * 24 + 8 : (time + 7) * 24 + 16, :] * total
        )

    for kind in range(2):
        for half in range(2):
            for y in range(4):
                rows_out[(kind * 2 + half) * 4 : (kind * 2 + half) * 4 + 4, y * 128 : y * 128 + 128] = own_out[
                    pl.ds(kind * 32 + half * 4 + y, 4, stride=8), :
                ]
    ordered = split_dot(rows_out[...], perm, 3, transposed=True)
    for target in range(32):
        spot, half = target // 2, target % 2
        lanes = slice(spot * 32, spot * 32 + 32)
        out_ref[target, 8:12, 0:32] = ordered[half * 4 : half * 4 + 4, lanes]
        out_ref[target, 8:12, 32:64] = ordered[8 + half * 4 : 12 + half * 4, lanes]

    def put(block, values):
        out_ref[2 * block, 0:8, :] = values[0:8]
        out_ref[2 * block + 1, 0:8, :] = values[8:16]

    own2 = cot2[2:6, 2:10, :, 128:256].reshape(512, 128).astype(F32)
    own1 = cot1[1:5, 1:9, :, 128:256].reshape(512, 128).astype(F32)
    own_a = act2[5:9, 5:13, :, 128:256].reshape(512, 128).astype(F32)
    turn2 = own2.T.astype(BF16)
    turn1 = own1.T.astype(BF16)
    turn_a = own_a.T.astype(BF16)
    zone = lax.broadcasted_iota(jnp.int32, (16, 128), 1)

    def lane_sum(values, lanes_zone, shift):
        total = jnp.zeros((16, 128), F32)
        for z in range(8):
            total = total + jnp.where(lanes_zone == (z + shift) % 8, values[z * 16 : z * 16 + 16], 0.0)
        return total

    packed = [None] * 11
    for first in range(3):
        for second in range(3):
            block = act1[5 + first : 9 + first, 5 + second : 13 + second].reshape(512, 384)
            product = jnp.dot(turn2, block, preferred_element_type=F32)
            for third in range(3):
                for ez in range(3):
                    number = ((first * 3 + second) * 3 + third) * 3 + ez
                    part = lane_sum(product[:, third * 128 : third * 128 + 128], zone // 16, ez - 1)
                    for step in (64, 32, 16):
                        part = part + pltpu.roll(part, step, 1)
                    old = packed[number // 8]
                    packed[number // 8] = (
                        part if old is None else jnp.where(zone // 16 == number % 8, part, old)
                    )
    for number in range(11):
        put(number, packed[number])

    extra = jnp.zeros((16, 128), F32)
    for first in range(3):
        block = third_x[2 + first : 6 + first, 2:10].reshape(512, 256)
        product = jnp.dot(turn_a, block, preferred_element_type=F32)
        total = jnp.zeros((16, 128), F32)
        for o in range(2):
            for ez in range(3):
                part = fold_group(lane_sum(product[:, o * 128 : o * 128 + 128], zone % 8, 1 - ez))
                total = jnp.where(zone % 8 == o * 3 + ez, part, total)
        block = frozen_x[6 + first : 10 + first, 6:14].reshape(512, 128)
        product = jnp.dot(turn1, block, preferred_element_type=F32)
        for ez in range(3):
            part = fold_group(lane_sum(product, zone % 8, ez - 1))
            if ez < 2:
                total = jnp.where(zone % 8 == 6 + ez, part, total)
            else:
                extra = jnp.where(zone % 8 == first, part, extra)
        put(11 + first, total)
    put(14, extra)
    sums = [
        jnp.sum(own1, axis=0, keepdims=True),
        jnp.sum(own2, axis=0, keepdims=True),
        jnp.sum(jnp.sum(scale_c[3:7], axis=0)[3:11], axis=0, keepdims=True),
        jnp.sum(jnp.sum(shift_c[3:7], axis=0)[3:11], axis=0, keepdims=True),
    ]
    site = lax.broadcasted_iota(jnp.int32, (16, 128), 0)
    total = jnp.zeros((16, 128), F32)
    for row, value in enumerate(sums):
        total = jnp.where(site == row, jnp.broadcast_to(value, (16, 128)), total)
    put(15, total)


def unpack_kernel(in_ref, flowed_ref, grad_ref, share_ref, window):
    total = in_ref[0, 0:8, :]
    for source in range(1, 32):
        total = total + in_ref[source, 0:8, :]
    for target in range(8):
        share_ref[target] = total
    for source in range(32):
        window[4 * source : 4 * source + 4, :] = in_ref[source, 8:12, :]
    turned = window[...].T
    flowed_ref[...] = turned[0:32]
    grad_ref[...] = turned[32:64]


def ring(count, step):
    return [(i, (i + step) % count) for i in range(count)]


def prepare_weights(kernel_one, kernel_two, kernel_three):
    circle = np.zeros((3, 8, 8), np.float32)
    for ez in range(3):
        for z in range(8):
            circle[ez, (z + ez - 1) % 8, z] = 1.0
    circle = jnp.asarray(circle, BF16)
    k1 = kernel_one[:, 0]
    w1 = jnp.einsum("oxyet,eab->tyxabo", k1[:, ::-1], circle).reshape(3, 72, 128)
    w1 = jnp.pad(w1, ((0, 0), (0, 56), (0, 0))).reshape(384, 128)
    k3f = kernel_three[:, :, :, ::-1, :, ::-1]
    w3t = jnp.einsum("cixyet,eba->tcyxabi", k3f, circle).reshape(6, 72, 128)
    w3t = jnp.pad(w3t, ((0, 0), (0, 56), (0, 0))).reshape(768, 128)
    k2a = kernel_two.transpose(5, 3, 2, 4, 1, 0).reshape(81, 16, 1, 16)
    k2a = jnp.broadcast_to(k2a, (81, 16, 8, 16)).reshape(81, 16, 128)
    k2f = kernel_two[:, :, ::-1, ::-1, :, ::-1]
    k2t = k2f.transpose(5, 3, 2, 4, 0, 1).reshape(81, 16, 1, 16)
    k2t = jnp.broadcast_to(k2t, (81, 16, 8, 16)).reshape(81, 16, 128)
    k3 = kernel_three.transpose(5, 3, 2, 4, 0, 1).reshape(81, 2, 16, 1)
    k3 = jnp.broadcast_to(k3, (81, 2, 16, 128))
    k1b = k1[:, ::-1, ::-1, :, ::-1].transpose(4, 2, 1, 3, 0).reshape(81, 16, 1)
    k1b = jnp.broadcast_to(k1b, (81, 16, 128))
    w2, w2t, w3, w1t = pl.pallas_call(
        weights_kernel,
        out_shape=[
            jax.ShapeDtypeStruct((3456, 128), BF16),
            jax.ShapeDtypeStruct((3456, 128), BF16),
            jax.ShapeDtypeStruct((3456, 256), BF16),
            jax.ShapeDtypeStruct((3456, 128), BF16),
        ],
        in_specs=[VMEM_SPEC] * 4,
        out_specs=[VMEM_SPEC] * 4,
        compiler_params=pltpu.CompilerParams(vmem_limit_bytes=20 * 2**20),
        cost_estimate=pl.CostEstimate(flops=10**6, bytes_accessed=8 * 10**6, transcendentals=0),
        name="weights",
    )(k2a, k2t, k3, k1b)
    return w1, w3t, w2, w2t, w3, w1t


def local(field, parity_mask, kernel_one, bias_one, kernel_two, bias_two, kernel_three, bias_three):
    packed = pl.pallas_call(
        pack_kernel,
        out_shape=jax.ShapeDtypeStruct((32, 16, 128), F32),
        in_specs=[VMEM_SPEC] * 2,
        out_specs=VMEM_SPEC,
        scratch_shapes=[pltpu.VMEM((144, 128), F32)],
        name="pack",
    )(field.reshape(32, 128), parity_mask.reshape(32, 128))
    own = lax.all_to_all(packed, GROUP, 0, 0)
    low = lax.ppermute(own, "gyh", ring(8, 1))
    high = lax.ppermute(own, "gyh", ring(8, -1))
    w1, w3t, w2, w2t, w3, w1t = prepare_weights(kernel_one, kernel_two, kernel_three)
    bias = jnp.stack(
        [
            jnp.tile(bias_one, 8),
            jnp.tile(bias_two, 8),
            jnp.broadcast_to(bias_three[0], (128,)),
            jnp.broadcast_to(bias_three[1], (128,)),
        ]
    )
    perm = jnp.asarray(lane_permutation(), BF16)
    result = pl.pallas_call(
        main_kernel,
        out_shape=jax.ShapeDtypeStruct((32, 16, 128), F32),
        in_specs=[VMEM_SPEC] * 11,
        out_specs=VMEM_SPEC,
        scratch_shapes=[
            pltpu.VMEM((6, 24, 512), F32),
            pltpu.VMEM((6, 24, 512), F32),
            pltpu.VMEM((432, 128), F32),
            pltpu.VMEM((432, 128), F32),
            pltpu.VMEM((18, 20, 16, 128), BF16),
            pltpu.VMEM((16, 20, 16, 384), BF16),
            pltpu.VMEM((14, 18, 16, 384), BF16),
            pltpu.VMEM((12, 16, 128), F32),
            pltpu.VMEM((12, 16, 128), F32),
            pltpu.VMEM((12, 16, 128), F32),
            pltpu.VMEM((10, 14, 128), F32),
            pltpu.VMEM((10, 14, 128), F32),
            pltpu.VMEM((10, 14, 128), F32),
            pltpu.VMEM((10, 12, 16, 256), BF16),
            pltpu.VMEM((8, 12, 16, 384), BF16),
            pltpu.VMEM((6, 10, 16, 384), BF16),
            pltpu.VMEM((64, 128), F32),
            pltpu.VMEM((16, 512), F32),
        ],
        compiler_params=pltpu.CompilerParams(vmem_limit_bytes=48 * 2**20),
        cost_estimate=pl.CostEstimate(flops=2 * 10**10, bytes_accessed=8 * 10**6, transcendentals=10**6),
        name="flow",
    )(low, own, high, perm, w1, w3t, w2, w2t, w3, w1t, bias)
    back = lax.all_to_all(result, GROUP, 0, 0)
    flowed, field_grad, share = pl.pallas_call(
        unpack_kernel,
        out_shape=[
            jax.ShapeDtypeStruct((32, 128), F32),
            jax.ShapeDtypeStruct((32, 128), F32),
            jax.ShapeDtypeStruct((8, 8, 128), F32),
        ],
        in_specs=[VMEM_SPEC],
        out_specs=[VMEM_SPEC] * 3,
        scratch_shapes=[pltpu.VMEM((128, 128), F32)],
        name="unpack",
    )(back)
    share = lax.all_to_all(share, "gyh", 0, 0)
    share = jnp.sum(share, axis=0) * (1.0 / VOLUME)
    total = lax.all_to_all(jnp.broadcast_to(share[None], (32, 8, 128)), GROUP, 0, 0).reshape(256, 128)
    grad_two = total[0:176].reshape(11, 16, 8, 16).transpose(0, 2, 1, 3).reshape(88, 16, 16)[:81]
    grad_kernel_two = grad_two.reshape(3, 3, 3, 3, 16, 16).transpose(4, 5, 2, 1, 3, 0)
    mixed = total[176:224].reshape(3, 16, 128)[:, :, :72].reshape(3, 16, 3, 3, 8)
    third = mixed[::-1, :, ::-1, :, 0:6].reshape(3, 16, 3, 3, 2, 3)
    grad_kernel_three = third.transpose(4, 1, 3, 2, 5, 0)
    last = total[224:240][:, :72].reshape(16, 3, 3, 8)[..., 0:3].transpose(3, 0, 1, 2)
    one = jnp.concatenate([mixed[..., 6:8], last[..., None]], axis=-1)
    grad_kernel_one = one[:, :, :, ::-1].transpose(1, 3, 2, 4, 0)[:, None]
    sums = total[240:244]
    grad_bias_one = jnp.sum(sums[0].reshape(8, 16), axis=0)
    grad_bias_two = jnp.sum(sums[1].reshape(8, 16), axis=0)
    grad_bias_three = jnp.sum(sums[2:4], axis=1)
    return (
        flowed.reshape(2, 4, 4, 128),
        field_grad.reshape(2, 4, 4, 128),
        grad_kernel_one,
        grad_bias_one,
        grad_kernel_two,
        grad_bias_two,
        grad_kernel_three,
        grad_bias_three,
    )


def solution(mesh):
    split = Mesh(mesh.devices.reshape(8, 8, 2, 2), ("gx", "gyh", "gyl", "gz"))
    block = P("gx", ("gyh", "gyl"), "gz", None)
    return jax.shard_map(
        local,
        mesh=split,
        in_specs=(block, block, P(), P(), P(), P(), P(), P()),
        out_specs=(block, block, P(), P(), P(), P(), P(), P()),
        check_vma=False,
    )
```

profile of v0, /device:TPU:1, one launch (start us, length us, event | category | flops | bytes accessed | tf_op | source)
XLA Modules:
  0.0 127.1 jit_solution(775495251961867585)
XLA Ops:
  0.7 1.6 %pack.1 = f32[32,16,128]{2,1,0:T(8,128)} custom-call(f32[32,128]{1,0:T(8,128)} %bitcast.91, s32[32,128]{1,0:T(8,128)} %bitcast.92), custom_call_target="tpu_custom_call" | custom-call | tf_op jit(solution)/shard_map/pack/pallas_call | solution.py:393
  2.3 9.9 %all-to-all-start = ((f32[32,16,128]{2,1,0:T(8,128)}), f32[32,16,128]{2,1,0:T(8,128)S(1)}, u32[]{:S(2)}, u32[]{:S(2)}) async-start(f32[32,16,128]{2,1,0:T(8,128)} %pack.1), calls=%async_computation | async-start | bytes 524288 | tf_op jit(solution)/shard_map/all_to_all | solution.py:401
  12.3 1.0 reverse_bitcast_fusion
  13.3 0.8 rev.18
  14.0 0.8 rev.19
  14.8 1.0 convolution_bitcast_fusion.1
  15.9 0.4 convolution_bitcast_fusion
  16.3 5.6 %all-to-all-done.own_ref = f32[32,16,128]{2,1,0:T(8,128)S(1)} async-done(((f32[32,16,128]{2,1,0:T(8,128)}), f32[32,16,128]{2,1,0:T(8,128)S(1)}, u32[]{:S(2)}, u32[]{:S(2)}) %all-to-all-start) | async-done | bytes 262176 | tf_op jit(solution)/shard_map/all_to_all | solution.py:401
  21.9 3.0 %collective-permute-start = (f32[32,16,128]{2,1,0:T(8,128)S(1)}, f32[32,16,128]{2,1,0:T(8,128)S(1)}, u32[]{:S(2)}, u32[]{:S(2)}) collective-permute-start(f32[32,16,128]{2,1,0:T(8,128)S(1)} %all-to-all-done.own_ref), channel_id=1, source_target_pairs={{0,4},{4,8},{8,12},{12,16},{16,20},{20,24},{24,28},{28,0},{1,5},{5... | collective-permute-start | bytes 786440 | tf_op jit(solution)/shard_map/ppermute | solution.py:402
  24.9 2.2 %collective-permute-start.1 = (f32[32,16,128]{2,1,0:T(8,128)S(1)}, f32[32,16,128]{2,1,0:T(8,128)S(1)}, u32[]{:S(2)}, u32[]{:S(2)}) collective-permute-start(f32[32,16,128]{2,1,0:T(8,128)S(1)} %all-to-all-done.own_ref), channel_id=1, source_target_pairs={{0,28},{4,0},{8,4},{12,8},{16,12},{20,16},{24,20},{28,24},{1,29},{... | collective-permute-start | bytes 786440 | tf_op jit(solution)/shard_map/ppermute | solution.py:403
  27.0 0.6 fusion.4
  28.2 0.4 copy.49.k2t_ref
  28.6 1.2 copy.42
  30.2 0.4 copy.48.k2_ref
  30.6 0.7 pad.14.clone
  31.3 0.7 pad.15.clone
  32.8 0.6 reshape.92
  33.7 0.4 broadcast_in_dim.45.k3_ref
  34.1 1.3 %weights.1 = (bf16[3456,128]{1,0:T(8,128)(2,1)S(1)}, bf16[3456,128]{1,0:T(8,128)(2,1)S(1)}, bf16[3456,256]{1,0:T(8,128)(2,1)S(1)}, bf16[3456,128]{1,0:T(8,128)(2,1)S(1)}) custom-call(bf16[81,16,128]{2,1,0:T(8,128)(2,1)S(1)} %copy.48.k2_ref, bf16[81,16,128]{2,1,0:T(8,128)(2,1)S(1)} %copy.49.k2t_ref, bf16[81,2,16,128]{3,2,1,0:T(8,128)(2,1)S(1)} %broadcast_in_dim.45.k3_ref, ...), custom_call_target="tpu_custom_call" | custom-call | flops 1000000 | bytes 8000000 | tf_op jit(solution)/shard_map/weights/pallas_call | solution.py:375
  35.5 1.2 copy-done
  36.8 3.7 %collective-permute-done.1.high_ref = f32[32,16,128]{2,1,0:T(8,128)S(1)} collective-permute-done((f32[32,16,128]{2,1,0:T(8,128)S(1)}, f32[32,16,128]{2,1,0:T(8,128)S(1)}, u32[]{:S(2)}, u32[]{:S(2)}) %collective-permute-start.1) | collective-permute-done | bytes 262176 | tf_op jit(solution)/shard_map/ppermute | solution.py:403
  40.4 40.1 %flow.1 = f32[32,16,128]{2,1,0:T(8,128)S(1)} custom-call(f32[32,16,128]{2,1,0:T(8,128)S(1)} %collective-permute-done.low_ref, f32[32,16,128]{2,1,0:T(8,128)S(1)} %all-to-all-done.own_ref, f32[32,16,128]{2,1,0:T(8,128)S(1)} %collective-permute-done.1.high_ref, bf16[512,512]{1,0:T(8,128)(2,1)S(1)} %copy-done.1, bf16[384,128]{1,0:T(8,128)(2,1)S(1)} %bitcast.68, ...), custom_call_target="tpu_custom_call" | custom-call | flops 20000000000 | bytes 8000000 | tf_op jit(solution)/shard_map/flow/pallas_call | solution.py:414
  80.5 13.7 %all_to_all.20.in_ref = f32[32,16,128]{2,1,0:T(8,128)} all-to-all(f32[32,16,128]{2,1,0:T(8,128)S(1)} %flow.1), channel_id=1, replica_groups=mesh['gx'=8,'gyh'=8,'gyl'=2,'gz'=2] {'gz','gx','gyl'}, dimensions={0} | all-to-all | bytes 524288 | tf_op jit(solution)/shard_map/all_to_all | solution.py:443
  94.2 1.7 %unpack.1 = (f32[32,128]{1,0:T(8,128)}, f32[32,128]{1,0:T(8,128)}, f32[8,8,128]{2,1,0:T(8,128)}) custom-call(f32[32,16,128]{2,1,0:T(8,128)} %all_to_all.20.in_ref), custom_call_target="tpu_custom_call" | custom-call | tf_op jit(solution)/shard_map/unpack/pallas_call | solution.py:444
  95.8 12.3 %all_to_all.21 = f32[8,8,128]{2,1,0:T(8,128)S(1)} all-to-all(f32[8,8,128]{2,1,0:T(8,128)} %get-tuple-element.21), channel_id=1, replica_groups=mesh['gx'=8,'gyh'=8,'gyl'=2,'gz'=2] {'gyh'}, dimensions={0} | all-to-all | bytes 65536 | tf_op jit(solution)/shard_map/all_to_all | solution.py:456
  108.1 14.1 %all_to_all.22 = f32[32,8,128]{2,1,0:T(8,128)S(1)} all-to-all(f32[32,8,128]{2,1,0:T(8,128)S(1)} %broadcast_in_dim.48), channel_id=1, replica_groups=mesh['gx'=8,'gyh'=8,'gyl'=2,'gz'=2] {'gz','gx','gyl'}, dimensions={0} | all-to-all | bytes 262144 | tf_op jit(solution)/shard_map/all_to_all | solution.py:458
  122.2 0.6 slice_reduce_fusion
  123.2 0.7 copy.55
  123.9 0.5 reduce_sum.37
  124.5 0.5 reduce_sum.38
  125.1 0.7 copy.57
  126.2 0.9 copy.56
  (58 shorter events, 3.1 us)
Async XLA Ops:
  0.6 15.2 %copy-start.4 = (bf16[3,8,8,1,1,1,1]{2,0,6,5,4,3,1:T(4,128)(2,1)S(1)}, bf16[3,8,8,1,1,1,1]{2,0,6,5,4,3,1:T(4,128)(2,1)}, u32[]{:S(2)}) copy-start(bf16[3,8,8,1,1,1,1]{2,0,6,5,4,3,1:T(4,128)(2,1)} %constant.20) | copy-start | bytes 1156
  0.6 27.0 %copy-start.3 = (bf16[16,1,3,3,3,3]{0,5,4,3,2,1:T(4,128)(2,1)S(1)}, bf16[16,1,3,3,3,3]{0,5,4,3,2,1:T(4,128)(2,1)}, u32[]{:S(2)}) copy-start(bf16[16,1,3,3,3,3]{0,5,4,3,2,1:T(4,128)(2,1)} %param.12) | copy-start | bytes 7780
  0.7 26.4 %copy-start.5 = (f32[2]{0:T(128)S(1)}, f32[2]{0:T(128)}, u32[]{:S(2)}) copy-start(f32[2]{0:T(128)} %param.17) | copy-start | bytes 28
  2.3 19.6 %all-to-all-start = ((f32[32,16,128]{2,1,0:T(8,128)}), f32[32,16,128]{2,1,0:T(8,128)S(1)}, u32[]{:S(2)}, u32[]{:S(2)}) async-start(f32[32,16,128]{2,1,0:T(8,128)} %pack.1), calls=%async_computation | async-start | bytes 524288 | tf_op jit(solution)/shard_map/all_to_all | solution.py:401
  21.9 14.9 %collective-permute-start = (f32[32,16,128]{2,1,0:T(8,128)S(1)}, f32[32,16,128]{2,1,0:T(8,128)S(1)}, u32[]{:S(2)}, u32[]{:S(2)}) collective-permute-start(f32[32,16,128]{2,1,0:T(8,128)S(1)} %all-to-all-done.own_ref), channel_id=1, source_target_pairs={{0,4},{4,8},{8,12},{12,16},{16,20},{20,24},{24,28},{28,0},{1,5},{5... | collective-permute-start | bytes 786440 | tf_op jit(solution)/shard_map/ppermute | solution.py:402
  24.9 15.5 %collective-permute-start.1 = (f32[32,16,128]{2,1,0:T(8,128)S(1)}, f32[32,16,128]{2,1,0:T(8,128)S(1)}, u32[]{:S(2)}, u32[]{:S(2)}) collective-permute-start(f32[32,16,128]{2,1,0:T(8,128)S(1)} %all-to-all-done.own_ref), channel_id=1, source_target_pairs={{0,28},{4,0},{8,4},{12,8},{16,12},{20,16},{24,20},{28,24},{1,29},{... | collective-permute-start | bytes 786440 | tf_op jit(solution)/shard_map/ppermute | solution.py:403
  28.2 2.3 %copy-start.2 = (bf16[2,16,3,3,3,3]{1,0,5,4,3,2:T(2,128)(2,1)S(1)}, bf16[2,16,3,3,3,3]{1,0,5,4,3,2:T(2,128)(2,1)}, u32[]{:S(2)}) copy-start(bf16[2,16,3,3,3,3]{1,0,5,4,3,2:T(2,128)(2,1)} %param.16) | copy-start | bytes 15556
  28.2 3.8 %copy-start.6 = (f32[16]{0:T(128)S(1)}, f32[16]{0:T(128)}, u32[]{:S(2)}) copy-start(f32[16]{0:T(128)} %param.13) | copy-start | bytes 196
  28.2 3.9 %copy-start.7 = (f32[16]{0:T(128)S(1)}, f32[16]{0:T(128)}, u32[]{:S(2)}) copy-start(f32[16]{0:T(128)} %param.15) | copy-start | bytes 196
  33.4 7.0 %copy-start.1 = (bf16[512,512]{1,0:T(8,128)(2,1)S(1)}, bf16[512,512]{1,0:T(8,128)(2,1)}, u32[]{:S(2)}) copy-start(bf16[512,512]{1,0:T(8,128)(2,1)} %constant.12.clone.perm_ref) | copy-start | bytes 1572868
  35.5 1.2 copy-start
where the time goes:
time: 128 us; the launch traced here: 127 us
  Pallas kernels  44.7 us (35%)
  blocking collectives  40 us (31%)
  starting transfers between devices  15.1 us (12%)
  local copies, waits for them, and re-layouts  13.8 us (11%)
  waiting for transfers between devices  9.26 us (7%)
  other arithmetic  1.82 us (1%)
  matrix products  1.45 us (1%)
    pallas_call x1, Pallas kernels, local(): pl.pallas_call(main_kernel, out_shape=jax.ShapeDtypeStruct((32, 16, 128),...  40.1 us
    all_to_all x1, blocking collectives, local(): lax.all_to_all(jnp.broadcast_to(share[None], (32, 8, 128)), GROUP, 0, 0)  14.1 us
    all_to_all x1, blocking collectives, local(): back = lax.all_to_all(result, GROUP, 0, 0)  13.7 us
    all_to_all x1, blocking collectives, local(): share = lax.all_to_all(share, 'gyh', 0, 0)  12.3 us
    all_to_all x1, starting transfers between devices, local(): own = lax.all_to_all(packed, GROUP, 0, 0)  9.94 us
    all_to_all x1, waiting for transfers between devices, local(): own = lax.all_to_all(packed, GROUP, 0, 0)  5.58 us
    ppermute x1, waiting for transfers between devices, local(): high = lax.ppermute(own, 'gyh', ring(8, -1))  3.67 us
    unnamed x20, local copies, waits for them, and re-layouts  3.48 us
  transfers between devices with their start and end apart: 3, of which 2 were waited for; matrix products, arithmetic and copies ran while one was open for 9% of the time, Pallas kernels for 1%

commit v1 on v0

v1 whole, which is shorter than its diff:
```python
import functools

import jax
import jax.numpy as jnp
import numpy as np
from jax import lax
from jax.experimental import pallas as pl
from jax.experimental.pallas import tpu as pltpu
from jax.sharding import Mesh
from jax.sharding import PartitionSpec as P

F32 = jnp.float32
BF16 = jnp.bfloat16
GROUP = ("gz", "gx", "gyl")
VMEM_SPEC = pl.BlockSpec(memory_space=pltpu.VMEM)
HBM_SPEC = pl.BlockSpec(memory_space=pltpu.HBM)
VOLUME = 1048576.0


def lane_permutation():
    matrix = np.zeros((512, 512), np.float32)
    for gz in range(2):
        for gx in range(8):
            for x in range(2):
                for y in range(4):
                    for z in range(4):
                        source = (gz * 8 + gx) * 32 + x * 16 + y * 4 + z
                        target = y * 128 + (gx * 2 + x) * 8 + gz * 4 + z
                        matrix[source, target] = 1.0
    return matrix


def split_kernel(field_ref, mask_ref, out_ref):
    field = field_ref[...]
    head = field.astype(BF16)
    out_ref[0:32, :] = head
    out_ref[32:64, :] = (field - head.astype(F32)).astype(BF16)
    out_ref[64:96, :] = mask_ref[...].astype(F32).astype(BF16)


def pack_kernel(low_ref, own_ref, high_ref, out_ref, window):
    empty = jnp.zeros((32, 128), F32)

    def turn(ref):
        both = ref[...].astype(F32)
        near = jnp.concatenate([pltpu.roll(both, 7, 1), empty], axis=0).T
        later = jnp.concatenate([empty, pltpu.roll(both, 119, 1)], axis=0).T
        return near, later

    low, low_later = turn(low_ref)
    own, own_later = turn(own_ref)
    high, high_later = turn(high_ref)
    lane = lax.broadcasted_iota(jnp.int32, (128, 128), 1)
    rows = [
        jnp.where(lane < 96, low, pltpu.roll(own, 96, 1)),
        jnp.where(lane < 64, pltpu.roll(own, 96, 1), pltpu.roll(high, 64, 1)),
        pltpu.roll(high, 64, 1),
        low_later,
        pltpu.roll(own_later, 2, 0),
        pltpu.roll(high_later, 4, 0),
    ]
    for number, value in enumerate(rows):
        window[number, 0:128, :] = value
        window[number, 128:144, :] = value[0:16, :]
    lane = lax.broadcasted_iota(jnp.int32, (16, 128), 1)
    row = lax.broadcasted_iota(jnp.int32, (16, 128), 0)
    for slot in range(32):
        here = slice(4 * slot, 4 * slot + 16)
        out_ref[slot, 0:16, :] = window[0, here, :].astype(BF16)
        out_ref[slot, 16:32, :] = window[1, here, :].astype(BF16)
        tail = jnp.where(row < 2, window[3, here, :], jnp.where(row < 4, window[4, here, :], window[5, here, :]))
        out_ref[slot, 32:48, :] = jnp.where(lane < 32, window[2, here, :], tail).astype(BF16)


def tile_dot(values):
    spot = lax.broadcasted_iota(jnp.int32, (16, 128), 0)
    lane = lax.broadcasted_iota(jnp.int32, (16, 128), 1)
    return jnp.dot(values, jnp.where(lane % 16 == spot, 1.0, 0.0).astype(BF16), preferred_element_type=F32)


def weights_kernel(
    k1_ref, k2_ref, k3_ref, b1_ref, b2_ref, b3_ref,
    w1_hbm, w3t_hbm, w2_hbm, w2t_hbm, w3_hbm, w1t_hbm, bias_hbm,
    w1_ref, w3t_ref, w2_ref, w2t_ref, w3_ref, w1t_ref, bias_ref, one, two, three, sems,
):
    def at(ex, ey, ez, et):
        return ((ex * 3 + ey) * 3 + ez) * 3 + et

    one[...] = tile_dot(k1_ref[...])
    two[...] = tile_dot(k2_ref[...])
    three[...] = tile_dot(k3_ref[...])
    zone = lax.broadcasted_iota(jnp.int32, (8, 128), 1) // 16
    spot = lax.broadcasted_iota(jnp.int32, (8, 128), 0)
    wide = lax.broadcasted_iota(jnp.int32, (16, 128), 1) // 16
    zeros = jnp.zeros((128, 128), BF16)

    def rows8(ref, base, ex, ey, et, ahead):
        total = jnp.zeros((8, 128), F32)
        for ez in range(3):
            value = jnp.broadcast_to(ref[base(at(ex, ey, ez, et)), :], (8, 128))
            total = jnp.where(zone == (spot + ahead * (ez - 1) + 8) % 8, value, total)
        return total

    def row_one(off):
        return slice(off, off + 1)

    def row_three(o):
        return lambda off: slice(off * 2 + o, off * 2 + o + 1)

    for et in range(3):
        w1_ref[et * 128 + 72 : et * 128 + 128, :] = jnp.zeros((56, 128), BF16)
        for ey in range(3):
            block = [rows8(one, row_one, 2 - turned, ey, et, -1) for turned in range(3)]
            w1_ref[et * 128 + ey * 24 : et * 128 + ey * 24 + 24, :] = jnp.concatenate(block, axis=0).astype(BF16)
        for o in range(2):
            base = (et * 2 + o) * 128
            w3t_ref[base + 72 : base + 128, :] = jnp.zeros((56, 128), BF16)
            for dy in range(3):
                block = [rows8(three, row_three(o), turned, 2 - dy, 2 - et, 1) for turned in range(3)]
                w3t_ref[base + dy * 24 : base + dy * 24 + 24, :] = jnp.concatenate(block, axis=0).astype(BF16)
        for ex in range(3):
            block = []
            for ey in range(3):
                for o in range(2):
                    block.append(rows8(three, row_three(o), ex, ey, et, 1))
            block.append(jnp.zeros((80, 128), F32))
            rows = slice((et * 3 + ex) * 128, (et * 3 + ex) * 128 + 128)
            w3_ref[rows, :] = jnp.concatenate(block, axis=0).T.astype(BF16)
            block = [rows8(one, row_one, 2 - ex, 2 - dy, 2 - et, -1) for dy in range(3)]
            block.append(jnp.zeros((104, 128), F32))
            w1t_ref[rows, :] = jnp.concatenate(block, axis=0).T.astype(BF16)
            for ey in range(3):
                parts = [two[at(ex, ey, ez, et) * 16 : at(ex, ey, ez, et) * 16 + 16, :] for ez in range(3)]
                block = []
                for z in range(8):
                    total = jnp.zeros((16, 128), F32)
                    for ez in range(3):
                        total = jnp.where(wide == (z + ez - 1) % 8, parts[ez], total)
                    block.append(total)
                block = jnp.concatenate(block, axis=0)
                turned = block.T.astype(BF16)
                block = block.astype(BF16)
                for member in range(2):
                    lanes = slice(member * 128, member * 128 + 128)
                    base = ((et * 4 + ey + member) * 3 + ex) * 128
                    w2_ref[base : base + 128, lanes] = turned
                    base = (((2 - et) * 4 + 2 - ey + member) * 3 + 2 - ex) * 128
                    w2t_ref[base : base + 128, lanes] = block
            for member in range(2):
                lanes = slice(member * 128, member * 128 + 128)
                base = ((et * 4 + 3 * (1 - member)) * 3 + ex) * 128
                w2_ref[base : base + 128, lanes] = zeros
                w2t_ref[base : base + 128, lanes] = zeros
    bias_ref[0:1, :] = jnp.concatenate([b1_ref[...]] * 8, axis=1)
    bias_ref[1:2, :] = jnp.concatenate([b2_ref[...]] * 8, axis=1)
    bias_ref[2:3, :] = jnp.broadcast_to(b3_ref[0:1, 0:1], (1, 128))
    bias_ref[3:4, :] = jnp.broadcast_to(b3_ref[0:1, 1:2], (1, 128))
    copies = []
    for number, (source, target) in enumerate(
        (
            (w1_ref, w1_hbm),
            (w3t_ref, w3t_hbm),
            (w2_ref, w2_hbm),
            (w2t_ref, w2t_hbm),
            (w3_ref, w3_hbm),
            (w1t_ref, w1t_hbm),
            (bias_ref, bias_hbm),
        )
    ):
        copies.append(pltpu.make_async_copy(source, target, sems.at[number]))
        copies[-1].start()
    for copy in copies:
        copy.wait()


def split_dot(values, matrix, parts, transposed=False):
    dims = (((1,), (1 if transposed else 0,)), ((), ()))
    total = None
    rest = values
    for _ in range(parts):
        head = rest.astype(BF16)
        rest = rest - head.astype(F32)
        term = lax.dot_general(head, matrix, dims, preferred_element_type=F32)
        total = term if total is None else total + term
    return total


def reverse_matrix():
    source = lax.broadcasted_iota(jnp.int32, (128, 128), 0)
    target = lax.broadcasted_iota(jnp.int32, (128, 128), 1)
    return jnp.where(source == (15 - target // 8) * 8 + target % 8, 1.0, 0.0).astype(BF16)


def spread_rows(values):
    count = values.shape[0] - 2
    site = lax.broadcasted_iota(jnp.int32, (count, 16, 128), 1)
    lane = (lax.broadcasted_iota(jnp.int32, (count, 16, 128), 2) + 8 * site) % 128
    pieces = []
    for second in range(3):
        turned = pltpu.roll(values, 16 + 24 * second, 1)[second : second + count]
        pieces.append(jnp.broadcast_to(turned[:, None, :], (count, 16, 128)))
    wide = jnp.where(lane < 24, pieces[0], jnp.where(lane < 48, pieces[1], pieces[2]))
    return pltpu.roll(wide, 0, 2, stride=8, stride_axis=1)


def gather_rows(values, place):
    count = values.shape[0]
    site = lax.broadcasted_iota(jnp.int32, (count, 16, 128), 1)
    lane = lax.broadcasted_iota(jnp.int32, (count, 16, 128), 2) // 8
    moved = pltpu.roll(values, 0, 2, stride=8, stride_axis=1)
    results = []
    for spot in range(place):
        total = jnp.sum(jnp.where(lane == (site + spot) % 16, moved, 0.0), axis=1)
        results.append(total if spot == 0 else pltpu.roll(total, 128 - 8 * spot, 1))
    return results


def shifted(values):
    return (
        pltpu.roll(values, 1, 1).astype(BF16),
        values.astype(BF16),
        pltpu.roll(values, 15, 1).astype(BF16),
    )


def pair_dot(ref, time, steps, pairs, w_ref):
    total = None
    for first in range(3):
        for block in range(4):
            rows = ref[pl.ds(time + first, steps), block // 2 : block // 2 + pairs, block % 2]
            rows = rows.reshape(steps * pairs * 16, 384)
            at = (first * 4 + block) * 384
            term = jnp.dot(rows, w_ref[at : at + 384, :], preferred_element_type=F32)
            total = term if total is None else total + term
    return total


def time_dot(ref, time, rows, w_ref):
    total = None
    for first in range(3):
        block = ref[time + first].reshape(rows, 384)
        term = jnp.dot(block, w_ref[first * 384 : first * 384 + 384, :], preferred_element_type=F32)
        total = term if total is None else total + term
    return total


def fold_group(values):
    lane = lax.broadcasted_iota(jnp.int32, values.shape, 1)
    for step in (1, 2, 4):
        down = pltpu.roll(values, 128 - step, 1)
        up = pltpu.roll(values, step, 1)
        values = values + jnp.where((lane // step) % 2 == 0, down, up)
    return values


def main_kernel(
    in_ref, perm_hbm, w1_hbm, w3t_hbm, w2_hbm, w2t_hbm, w3_hbm, bias_hbm,
    out_ref, cot1_hbm, held,
    gather, dense_f, dense_m, dense_z, frozen, frozen_x, act1, act2, pre0, pre1, flow, scale_c, shift_c,
    direct, third_x, cot2, cot1, perm_ref, w1_ref, w3t_ref, w2_ref, w2t_ref, w3_ref, bias_ref, sems,
):
    copies = {}
    for number, (name, source, target) in enumerate(
        (
            ("perm", perm_hbm, perm_ref),
            ("w1", w1_hbm, w1_ref),
            ("bias", bias_hbm, bias_ref),
            ("w2", w2_hbm, w2_ref),
            ("w3", w3_hbm, w3_ref),
            ("w3t", w3t_hbm, w3t_ref),
            ("w2t", w2t_hbm, w2t_ref),
        )
    ):
        copies[name] = pltpu.make_async_copy(source, target, sems.at[number])
        copies[name].start()

    def repeat(count, body):
        for step in range(count):
            body(step)

    for source in range(32):
        spot, half = source // 2, source % 2
        lanes = slice(spot * 32, spot * 32 + 32)
        tiles = [in_ref[source, 16 * tile : 16 * tile + 16, :].astype(F32) for tile in range(3)]
        for block in range(3):
            for kind in range(3):
                piece = block * 3 + kind
                at = piece % 4 * 32
                gather[kind * 6 + block * 2 + half, 0:16, lanes] = tiles[piece // 4][:, at : at + 32]
                at = 32 + 32 * kind
                gather[kind * 6 + block * 2 + half, 16:18, lanes] = tiles[2][2 * block : 2 * block + 2, at : at + 32]
    copies["perm"].wait()
    ordered = jnp.dot(
        gather[...].reshape(432, 512).astype(BF16), perm_ref[...], preferred_element_type=F32
    )
    for block in range(6):
        head = ordered[block * 24 : block * 24 + 18]
        rest = ordered[144 + block * 24 : 144 + block * 24 + 18]
        share = ordered[288 + block * 24 : 288 + block * 24 + 18]
        for y in range(4):
            lanes = slice(y * 128, y * 128 + 128)
            rows = pl.ds(block * 4 + y, 18, stride=24)
            dense_f[rows, :] = head[:, lanes] + rest[:, lanes]
            dense_m[rows, :] = share[:, lanes]
            dense_z[rows, :] = head[:, lanes] * share[:, lanes]
    reverse = reverse_matrix()
    frozen[...] = jnp.dot(dense_z[...].astype(BF16), reverse, preferred_element_type=F32)

    def spread_frozen(time):
        rows = slice(time * 24, time * 24 + 24)
        frozen_x[time] = spread_rows(frozen[rows, :][1:23]).astype(BF16)

    repeat(18, spread_frozen)

    copies["w1"].wait()
    copies["bias"].wait()

    def first_layer(time):
        total = bias_ref[0:1, :]
        for first in range(3):
            block = frozen_x[time + first].reshape(320, 128)
            total = total + jnp.dot(
                block, w1_ref[first * 128 : first * 128 + 128, :], preferred_element_type=F32
            )
        for third, part in enumerate(shifted(jnp.tanh(total).reshape(20, 16, 128))):
            act1[time, :, :, :, third * 128 : third * 128 + 128] = part.reshape(10, 2, 16, 128)

    repeat(16, first_layer)

    copies["w2"].wait()

    def second_layer(step):
        total = pair_dot(act1, step * 2, 2, 9, w2_ref)
        for member in range(2):
            values = jnp.tanh(total[:, member * 128 : member * 128 + 128] + bias_ref[1:2, :])
            for third, part in enumerate(shifted(values.reshape(18, 16, 128))):
                act2[pl.ds(step * 2, 2), :, member, :, third * 128 : third * 128 + 128] = part.reshape(2, 9, 16, 128)

    repeat(7, second_layer)

    copies["w3"].wait()

    def third_layer(time):
        total = time_dot(act2, time, 288, w3_ref).reshape(18, 16, 128)
        total = total[0:16] + pltpu.roll(total[1:17], 112, 2) + pltpu.roll(total[2:18], 96, 2)
        scale, shift = gather_rows(total, 2)
        pre0[time] = scale + bias_ref[2:3, :]
        pre1[time] = shift + bias_ref[3:4, :]

    repeat(12, third_layer)

    def transform(time):
        rows = slice((time + 3) * 24, (time + 3) * 24 + 24)
        field = dense_f[rows, :][4:20]
        share = dense_m[rows, :][4:20]
        growth = jnp.exp(jnp.tanh(pre0[time]))
        flow[time] = share * field + (1.0 - share) * (field * growth + pre1[time])

    repeat(12, transform)

    def force_step(time):
        rows = slice((time + 4) * 24, (time + 4) * 24 + 24)
        field = dense_f[rows, :][5:19]
        share = dense_m[rows, :][5:19]
        here = flow[time + 1]
        lane = lax.broadcasted_iota(jnp.int32, (16, 128), 1) % 8
        around = flow[time] + flow[time + 2] + pltpu.roll(here, 8, 1) + pltpu.roll(here, 120, 1)
        around = around + jnp.where(lane == 0, pltpu.roll(here, 121, 1), pltpu.roll(here, 1, 1))
        around = around + jnp.where(lane == 7, pltpu.roll(here, 7, 1), pltpu.roll(here, 127, 1))
        around = around[1:15] + here[0:14] + here[2:16]
        mid = here[1:15]
        force = -0.5 * around + 1.8 * mid + 0.2 * mid * mid * mid
        scale = jnp.tanh(pre0[time + 1][1:15])
        growth = jnp.exp(scale)
        active = 1.0 - share
        empty = jnp.zeros((2, 128), F32)
        scale_c[time] = jnp.concatenate(
            [active * (force * field * growth - 1.0) * (1.0 - scale * scale), empty], axis=0
        )
        shift_c[time] = jnp.concatenate([active * force, empty], axis=0)
        direct[time] = force * (share + active * growth)

    repeat(10, force_step)
    scale_c[...] = jnp.dot(
        scale_c[...].reshape(160, 128).astype(BF16), reverse, preferred_element_type=F32
    ).reshape(10, 16, 128)
    shift_c[...] = jnp.dot(
        shift_c[...].reshape(160, 128).astype(BF16), reverse, preferred_element_type=F32
    ).reshape(10, 16, 128)

    def spread_third(time):
        third_x[time, :, :, 0:128] = spread_rows(scale_c[time][0:14]).astype(BF16)
        third_x[time, :, :, 128:256] = spread_rows(shift_c[time][0:14]).astype(BF16)

    repeat(10, spread_third)

    copies["w3t"].wait()

    def second_cot(time):
        total = None
        for first in range(3):
            block = third_x[time + first].reshape(192, 256)
            term = jnp.dot(
                block, w3t_ref[first * 256 : first * 256 + 256, :], preferred_element_type=F32
            )
            total = term if total is None else total + term
        act = act2[time + 3, :, :, :, 128:256].reshape(18, 16, 128)[3:15].astype(F32)
        values = total.reshape(12, 16, 128) * (1.0 - act * act)
        for third, part in enumerate(shifted(values)):
            cot2[time, :, :, :, third * 128 : third * 128 + 128] = part.reshape(6, 2, 16, 128)

    repeat(8, second_cot)

    copies["w2t"].wait()

    def first_cot(step):
        total = pair_dot(cot2, step * 2, 2, 5, w2t_ref)
        for member in range(2):
            act = act1[pl.ds(step * 2 + 5, 2), 2 + member : 7 + member, 1 - member, :, 128:256]
            act = act.astype(F32).reshape(10, 16, 128)
            values = total[:, member * 128 : member * 128 + 128].reshape(10, 16, 128) * (1.0 - act * act)
            for third, part in enumerate(shifted(values)):
                cot1[pl.ds(step * 2, 2), :, member, :, third * 128 : third * 128 + 128] = part.reshape(2, 5, 16, 128)

    repeat(3, first_cot)

    sent = pltpu.make_async_copy(cot1, cot1_hbm, sems.at[7])
    sent.start()
    for time in range(4):
        rows = slice(time * 8, time * 8 + 8)
        held[0, rows, :] = flow[time + 4][4:12]
        held[1, rows, :] = direct[time + 3][3:11]
        held[2, rows, :] = dense_m[(time + 7) * 24 + 8 : (time + 7) * 24 + 16, :]

    def put(block, values):
        out_ref[2 * block, :, :] = values[0:8]
        out_ref[2 * block + 1, :, :] = values[8:16]

    own2 = cot2[2:6, 1:5, :, :, 128:256].reshape(512, 128).astype(F32)
    own1 = cot1[1:5, :, :, :, 128:256].reshape(4, 10, 16, 128)[:, 1:9].reshape(512, 128).astype(F32)
    own_a = act2[5:9, :, :, :, 128:256].reshape(4, 18, 16, 128)[:, 5:13].reshape(512, 128).astype(F32)
    turn2 = own2.T.astype(BF16)
    turn1 = own1.T.astype(BF16)
    turn_a = own_a.T.astype(BF16)
    zone = lax.broadcasted_iota(jnp.int32, (16, 128), 1)

    def lane_sum(values, lanes_zone, shift):
        total = jnp.zeros((16, 128), F32)
        for z in range(8):
            total = total + jnp.where(lanes_zone == (z + shift) % 8, values[z * 16 : z * 16 + 16], 0.0)
        return total

    packed = [None] * 11
    for first in range(3):
        for second in range(3):
            low = (5 + second) // 2
            block = act1[5 + first : 9 + first, low : low + 5].reshape(4, 10, 16, 384)
            start = 5 + second - 2 * low
            block = block[:, start : start + 8].reshape(512, 384)
            product = jnp.dot(turn2, block, preferred_element_type=F32)
            for third in range(3):
                for ez in range(3):
                    number = ((third * 3 + second) * 3 + ez) * 3 + first
                    part = lane_sum(product[:, third * 128 : third * 128 + 128], zone // 16, ez - 1)
                    for step in (64, 32, 16):
                        part = part + pltpu.roll(part, step, 1)
                    old = packed[number // 8]
                    packed[number // 8] = (
                        part if old is None else jnp.where(zone // 16 == number % 8, part, old)
                    )
    for number in range(11):
        put(number, packed[number])

    extra = jnp.zeros((16, 128), F32)
    for first in range(3):
        block = third_x[2 + first : 6 + first, 2:10].reshape(512, 256)
        product = jnp.dot(turn_a, block, preferred_element_type=F32)
        total = jnp.zeros((16, 128), F32)
        for o in range(2):
            for ez in range(3):
                part = fold_group(lane_sum(product[:, o * 128 : o * 128 + 128], zone % 8, 1 - ez))
                total = jnp.where(zone % 8 == o * 3 + ez, part, total)
        block = frozen_x[6 + first : 10 + first, 6:14].reshape(512, 128)
        product = jnp.dot(turn1, block, preferred_element_type=F32)
        for ez in range(3):
            part = fold_group(lane_sum(product, zone % 8, ez - 1))
            if ez < 2:
                total = jnp.where(zone % 8 == 6 + ez, part, total)
            else:
                extra = jnp.where(zone % 8 == first, part, extra)
        put(11 + first, total)
    put(14, extra)
    sums = [
        jnp.sum(own1, axis=0, keepdims=True),
        jnp.sum(own2, axis=0, keepdims=True),
        jnp.sum(jnp.sum(scale_c[3:7], axis=0)[3:11], axis=0, keepdims=True),
        jnp.sum(jnp.sum(shift_c[3:7], axis=0)[3:11], axis=0, keepdims=True),
    ]
    site = lax.broadcasted_iota(jnp.int32, (16, 128), 0)
    total = jnp.zeros((16, 128), F32)
    for row, value in enumerate(sums):
        total = jnp.where(site == row, jnp.broadcast_to(value, (16, 128)), total)
    put(15, total)
    sent.wait()


def input_grad_kernel(
    cot1_hbm, held_ref, w1t_hbm, perm_hbm, out_ref, own_out, rows_out, cot1_ref, w1t_ref, perm_ref, sems
):
    copies = [
        pltpu.make_async_copy(cot1_hbm, cot1_ref, sems.at[0]),
        pltpu.make_async_copy(w1t_hbm, w1t_ref, sems.at[1]),
        pltpu.make_async_copy(perm_hbm, perm_ref, sems.at[2]),
    ]
    for copy in copies:
        copy.start()
    for copy in copies:
        copy.wait()
    for time in range(4):
        total = time_dot(cot1_ref, time, 160, w1t_ref).reshape(10, 16, 128)
        total = total[0:8] + pltpu.roll(total[1:9], 120, 2) + pltpu.roll(total[2:10], 112, 2)
        (total,) = gather_rows(total, 1)
        rows = slice(time * 8, time * 8 + 8)
        own_out[rows, :] = held_ref[0, rows, :]
        own_out[32 + time * 8 : 40 + time * 8, :] = held_ref[1, rows, :] + held_ref[2, rows, :] * total
    for kind in range(2):
        for half in range(2):
            for y in range(4):
                rows_out[(kind * 2 + half) * 4 : (kind * 2 + half) * 4 + 4, y * 128 : y * 128 + 128] = own_out[
                    pl.ds(kind * 32 + half * 4 + y, 4, stride=8), :
                ]
    ordered = split_dot(rows_out[...], perm_ref[...], 3, transposed=True)
    for target in range(32):
        spot, half = target // 2, target % 2
        lanes = slice(spot * 32, spot * 32 + 32)
        out_ref[target] = jnp.zeros((8, 128), F32)
        out_ref[target, 0:4, 0:32] = ordered[half * 4 : half * 4 + 4, lanes]
        out_ref[target, 0:4, 32:64] = ordered[8 + half * 4 : 12 + half * 4, lanes]


def unpack_kernel(in_ref, flowed_ref, grad_ref, g1_ref, g2_ref, g3_ref, b1_ref, b2_ref, b3_ref, window, extra, turned_x):
    for source in range(32):
        window[4 * source : 4 * source + 4, :] = in_ref[source, 8:12, :]
    turned = window[...].T
    flowed_ref[...] = turned[0:32]
    grad_ref[...] = turned[32:64]

    def group(number):
        return jnp.concatenate([in_ref[2 * number, 0:8, :], in_ref[2 * number + 1, 0:8, :]], axis=0)

    for number in range(11):
        block = group(number)
        for slot in range(min(8, 81 - number * 8)):
            g2_ref[number * 8 + slot] = block[:, slot * 16 : slot * 16 + 16]
    for number in range(4):
        extra[number * 16 : number * 16 + 16, :] = group(11 + number)
    extra[64:128, :] = jnp.zeros((64, 128), F32)
    turned_x[...] = extra[...].T
    for et in range(3):
        lanes = slice(et * 16, et * 16 + 16)
        for ey in range(3):
            for ex in range(3):
                for ez in range(3):
                    off = ((ex * 3 + ey) * 3 + ez) * 3
                    row = ey * 24 + (2 - ex) * 8
                    if ez < 2:
                        g1_ref[off + et] = turned_x[row + 6 + ez : row + 7 + ez, lanes]
                    else:
                        g1_ref[off + et] = turned_x[row + et : row + et + 1, 48:64]
                    row = (2 - ey) * 24 + ex * 8 + ez
                    g3_ref[off + 2 - et, 0:1, :] = turned_x[row : row + 1, lanes]
                    g3_ref[off + 2 - et, 1:2, :] = turned_x[row + 3 : row + 4, lanes]
    sums = in_ref[30, 0:8, :]
    lane = lax.broadcasted_iota(jnp.int32, (1, 128), 1)
    total = jnp.sum(sums, axis=1, keepdims=True)
    b3_ref[...] = jnp.where(lane == 0, total[2:3], total[3:4])[:, 0:2]
    for step in (64, 32, 16):
        sums = sums + pltpu.roll(sums, step, 1)
    b1_ref[...] = sums[0:1, 0:16]
    b2_ref[...] = sums[1:2, 0:16]


def ring(count, step):
    return [(i, (i + step) % count) for i in range(count)]


def shape(dims, dtype=F32):
    return jax.ShapeDtypeStruct(dims, dtype)


def run_weights(kernel_one, bias_one, kernel_two, bias_two, kernel_three, bias_three):
    return pl.pallas_call(
        weights_kernel,
        out_shape=[
            shape((384, 128), BF16),
            shape((768, 128), BF16),
            shape((4608, 256), BF16),
            shape((4608, 256), BF16),
            shape((1152, 128), BF16),
            shape((1152, 128), BF16),
            shape((4, 128)),
        ],
        in_specs=[VMEM_SPEC] * 6,
        out_specs=[HBM_SPEC] * 7,
        scratch_shapes=[
            pltpu.VMEM((384, 128), BF16),
            pltpu.VMEM((768, 128), BF16),
            pltpu.VMEM((4608, 256), BF16),
            pltpu.VMEM((4608, 256), BF16),
            pltpu.VMEM((1152, 128), BF16),
            pltpu.VMEM((1152, 128), BF16),
            pltpu.VMEM((4, 128), F32),
            pltpu.VMEM((81, 128), F32),
            pltpu.VMEM((1296, 128), F32),
            pltpu.VMEM((162, 128), F32),
            pltpu.SemaphoreType.DMA((7,)),
        ],
        compiler_params=pltpu.CompilerParams(vmem_limit_bytes=60 * 2**20),
        cost_estimate=pl.CostEstimate(flops=10**6, bytes_accessed=8 * 10**6, transcendentals=0),
        name="weights",
    )(
        kernel_one[:, 0].transpose(1, 2, 3, 4, 0).reshape(81, 16),
        kernel_two.transpose(2, 3, 4, 5, 0, 1).reshape(1296, 16),
        kernel_three.transpose(2, 3, 4, 5, 0, 1).reshape(162, 16),
        bias_one.reshape(1, 16),
        bias_two.reshape(1, 16),
        bias_three.reshape(1, 2),
    )


def run_main(*operands, name="flow"):
    return pl.pallas_call(
        main_kernel,
        out_shape=[
            shape((32, 8, 128)),
            shape((6, 5, 2, 16, 384), BF16),
            shape((3, 32, 128)),
        ],
        in_specs=[VMEM_SPEC] + [HBM_SPEC] * 7,
        out_specs=[VMEM_SPEC, HBM_SPEC, VMEM_SPEC],
        scratch_shapes=[
            pltpu.VMEM((18, 24, 512), F32),
            pltpu.VMEM((432, 128), F32),
            pltpu.VMEM((432, 128), F32),
            pltpu.VMEM((432, 128), F32),
            pltpu.VMEM((432, 128), F32),
            pltpu.VMEM((18, 20, 16, 128), BF16),
            pltpu.VMEM((16, 10, 2, 16, 384), BF16),
            pltpu.VMEM((14, 9, 2, 16, 384), BF16),
            pltpu.VMEM((12, 16, 128), F32),
            pltpu.VMEM((12, 16, 128), F32),
            pltpu.VMEM((12, 16, 128), F32),
            pltpu.VMEM((10, 16, 128), F32),
            pltpu.VMEM((10, 16, 128), F32),
            pltpu.VMEM((10, 14, 128), F32),
            pltpu.VMEM((10, 12, 16, 256), BF16),
            pltpu.VMEM((8, 6, 2, 16, 384), BF16),
            pltpu.VMEM((6, 5, 2, 16, 384), BF16),
            pltpu.VMEM((512, 512), BF16),
            pltpu.VMEM((384, 128), BF16),
            pltpu.VMEM((768, 128), BF16),
            pltpu.VMEM((4608, 256), BF16),
            pltpu.VMEM((4608, 256), BF16),
            pltpu.VMEM((1152, 128), BF16),
            pltpu.VMEM((4, 128), F32),
            pltpu.SemaphoreType.DMA((8,)),
        ],
        compiler_params=pltpu.CompilerParams(vmem_limit_bytes=60 * 2**20),
        cost_estimate=pl.CostEstimate(flops=2 * 10**10, bytes_accessed=8 * 10**6, transcendentals=10**6),
        name=name,
    )(*operands)


def main_shapes():
    return [
        shape((32, 48, 128), BF16), shape((512, 512), BF16), shape((384, 128), BF16), shape((768, 128), BF16),
        shape((4608, 256), BF16), shape((4608, 256), BF16), shape((1152, 128), BF16), shape((4, 128)),
    ]


def local(field, parity_mask, kernel_one, bias_one, kernel_two, bias_two, kernel_three, bias_three):
    own = pl.pallas_call(
        split_kernel,
        out_shape=shape((96, 128), BF16),
        in_specs=[VMEM_SPEC] * 2,
        out_specs=VMEM_SPEC,
        name="split",
    )(field.reshape(32, 128), parity_mask.reshape(32, 128))
    low = lax.ppermute(own, "gyh", ring(8, 1))
    high = lax.ppermute(own, "gyh", ring(8, -1))
    packed = pl.pallas_call(
        pack_kernel,
        out_shape=shape((32, 48, 128), BF16),
        in_specs=[VMEM_SPEC] * 3,
        out_specs=VMEM_SPEC,
        scratch_shapes=[pltpu.VMEM((6, 144, 128), F32)],
        name="pack",
    )(low, own, high)
    gathered = lax.all_to_all(packed, GROUP, 0, 0)
    w1, w3t, w2, w2t, w3, w1t, bias = run_weights(
        kernel_one, bias_one, kernel_two, bias_two, kernel_three, bias_three
    )
    perm = jnp.asarray(lane_permutation(), BF16)
    shares, cot1, held = run_main(gathered, perm, w1, w3t, w2, w2t, w3, bias)
    shares = lax.all_to_all(shares, GROUP, 0, 0)
    outputs = pl.pallas_call(
        input_grad_kernel,
        out_shape=shape((32, 8, 128)),
        in_specs=[HBM_SPEC, VMEM_SPEC, HBM_SPEC, HBM_SPEC],
        out_specs=VMEM_SPEC,
        scratch_shapes=[
            pltpu.VMEM((64, 128), F32),
            pltpu.VMEM((16, 512), F32),
            pltpu.VMEM((6, 5, 2, 16, 384), BF16),
            pltpu.VMEM((1152, 128), BF16),
            pltpu.VMEM((512, 512), BF16),
            pltpu.SemaphoreType.DMA((3,)),
        ],
        compiler_params=pltpu.CompilerParams(vmem_limit_bytes=60 * 2**20),
        cost_estimate=pl.CostEstimate(flops=5 * 10**8, bytes_accessed=3 * 10**6, transcendentals=0),
        name="input_grad",
    )(cot1, held, w1t, perm)
    share = jnp.broadcast_to(jnp.sum(shares, axis=0)[None], (8, 8, 128))
    share = lax.all_to_all(share, "gyh", 0, 0)
    share = jnp.sum(share, axis=0) * (1.0 / VOLUME)
    last = jnp.concatenate([jnp.broadcast_to(share[None], (32, 8, 128)), outputs], axis=1)
    last = lax.all_to_all(last, GROUP, 0, 0)
    flowed, field_grad, g1, g2, g3, b1, b2, b3 = pl.pallas_call(
        unpack_kernel,
        out_shape=[
            shape((32, 128)), shape((32, 128)), shape((81, 1, 16)), shape((81, 16, 16)), shape((81, 2, 16)),
            shape((1, 16)), shape((1, 16)), shape((1, 2)),
        ],
        in_specs=[VMEM_SPEC],
        out_specs=[VMEM_SPEC] * 8,
        scratch_shapes=[pltpu.VMEM((128, 128), F32), pltpu.VMEM((128, 128), F32), pltpu.VMEM((128, 128), F32)],
        name="unpack",
    )(last)
    return (
        flowed.reshape(2, 4, 4, 128),
        field_grad.reshape(2, 4, 4, 128),
        g1.reshape(3, 3, 3, 3, 1, 16).transpose(5, 4, 0, 1, 2, 3),
        b1.reshape(16),
        g2.reshape(3, 3, 3, 3, 16, 16).transpose(4, 5, 0, 1, 2, 3),
        b2.reshape(16),
        g3.reshape(3, 3, 3, 3, 2, 16).transpose(4, 5, 0, 1, 2, 3),
        b3.reshape(2),
    )


def solution(mesh):
    split = Mesh(mesh.devices.reshape(8, 8, 2, 2), ("gx", "gyh", "gyl", "gz"))
    block = P("gx", ("gyh", "gyl"), "gz", None)
    return jax.shard_map(
        local,
        mesh=split,
        in_specs=(block, block, P(), P(), P(), P(), P(), P()),
        out_specs=(block, block, P(), P(), P(), P(), P(), P()),
        check_vma=False,
    )
```

time: 128 us -> 105 us (0.82)
  blocking collectives: 40 us -> 28.1 us
  local copies, waits for them, and re-layouts: 13.8 us -> 4.83 us
  Pallas kernels: 44.7 us -> 36 us
  starting transfers between devices: 15.1 us -> 20.5 us
  waiting for transfers between devices: 9.26 us -> 12.8 us
  matrix products: 1.45 us -> 0 us
    all_to_all x3 -> x2, blocking collectives: 40 us -> 28.1 us  [the longest x1 14.8 us: local(): last = lax.all_to_all(last, GROUP, 0, 0)]
    pallas_call x4 -> x6, Pallas kernels: 44.7 us -> 36 us  [the longest x1 22 us: run_main(): pl.pallas_call(main_kernel, out_shape=[shape((32, 8, 128)), shape((6, 5,...]
    ppermute x1, starting transfers between devices: 2.16 us -> 7.78 us  [local(): high = lax.ppermute(own, 'gyh', ring(8, -1))]
    ppermute x1, waiting for transfers between devices: 0.01 us -> 4.75 us  [local(): low = lax.ppermute(own, 'gyh', ring(8, 1))]
    ppermute x1, starting transfers between devices: 2.99 us -> 0.01 us  [local(): low = lax.ppermute(own, 'gyh', ring(8, 1))]
    all_to_all x1 -> x2, starting transfers between devices: 9.94 us -> 12.7 us  [the longest x1 9.34 us: local(): gathered = lax.all_to_all(packed, GROUP, 0, 0)]
    transpose x8 -> x0, local copies, waits for them, and re-layouts: 2.71 us -> none  [the longest x1 1.17 us: prepare_weights(): k2a = kernel_two.transpose(5, 3, 2, 4, 1, 0).reshape(81, 16, 1, 16)]
    ppermute x1, waiting for transfers between devices: 3.67 us -> 1.15 us  [local(): high = lax.ppermute(own, 'gyh', ring(8, -1))]
  transfers between devices with their start and end apart: 3 -> 4, of which waited for: 2 -> 4; matrix products, arithmetic and copies ran while one was open for 9% -> 3% of each run, Pallas kernels for 1% -> 8%
where the time goes in v1:
time: 105 us; the launch traced here: 104 us
  Pallas kernels  36 us (34%)
  blocking collectives  28.1 us (27%)
  starting transfers between devices  20.5 us (20%)
  waiting for transfers between devices  12.8 us (12%)
  local copies, waits for them, and re-layouts  4.83 us (5%)
    pallas_call x1, Pallas kernels, run_main(): pl.pallas_call(main_kernel, out_shape=[shape((32, 8, 128)), shape((6, 5,...  22 us
    all_to_all x1, blocking collectives, local(): last = lax.all_to_all(last, GROUP, 0, 0)  14.8 us
    all_to_all x1, blocking collectives, local(): shares = lax.all_to_all(shares, GROUP, 0, 0)  13.4 us
    all_to_all x1, starting transfers between devices, local(): gathered = lax.all_to_all(packed, GROUP, 0, 0)  9.34 us
    ppermute x1, starting transfers between devices, local(): high = lax.ppermute(own, 'gyh', ring(8, -1))  7.78 us
    ppermute x1, waiting for transfers between devices, local(): low = lax.ppermute(own, 'gyh', ring(8, 1))  4.75 us
    pallas_call x1, Pallas kernels, run_weights(): pl.pallas_call(weights_kernel, out_shape=[shape((384, 128), BF16), shape(...  4.35 us
    pallas_call x1, Pallas kernels, local(): pl.pallas_call(input_grad_kernel, out_shape=shape((32, 8, 128)), in_specs...  4.1 us
  transfers between devices with their start and end apart: 4, of which 4 were waited for; matrix products, arithmetic and copies ran while one was open for 3% of the time, Pallas kernels for 8%

profile of v1, /device:TPU:1, one launch (start us, length us, event | category | flops | bytes accessed | tf_op | source)
XLA Modules:
  0.0 103.9 jit_solution(1744349241529367032)
XLA Ops:
  0.6 1.3 %split.1.own_ref = bf16[96,128]{1,0:T(8,128)(2,1)} custom-call(f32[32,128]{1,0:T(8,128)} %bitcast.29, s32[32,128]{1,0:T(8,128)} %bitcast.30), custom_call_target="tpu_custom_call" | custom-call | tf_op jit(solution)/shard_map/split/pallas_call | solution.py:682
  2.0 7.8 %collective-permute-start.1 = (bf16[96,128]{1,0:T(8,128)(2,1)}, bf16[96,128]{1,0:T(8,128)(2,1)S(1)}, u32[]{:S(2)}, u32[]{:S(2)}) collective-permute-start(bf16[96,128]{1,0:T(8,128)(2,1)} %split.1.own_ref), channel_id=1, source_target_pairs={{0,28},{4,0},{8,4},{12,8},{16,12},{20,16},{24,20},{28,24},{1,29},{... | collective-permute-start | bytes 73736 | tf_op jit(solution)/shard_map/ppermute | solution.py:690
  9.8 0.0 collective-permute-start
  9.8 1.2 %collective-permute-done.1.high_ref = bf16[96,128]{1,0:T(8,128)(2,1)S(1)} collective-permute-done((bf16[96,128]{1,0:T(8,128)(2,1)}, bf16[96,128]{1,0:T(8,128)(2,1)S(1)}, u32[]{:S(2)}, u32[]{:S(2)}) %collective-permute-start.1) | collective-permute-done | bytes 24608 | tf_op jit(solution)/shard_map/ppermute | solution.py:690
  10.9 0.0 copy-start.1
  10.9 4.7 %collective-permute-done.low_ref = bf16[96,128]{1,0:T(8,128)(2,1)S(1)} collective-permute-done((bf16[96,128]{1,0:T(8,128)(2,1)}, bf16[96,128]{1,0:T(8,128)(2,1)S(1)}, u32[]{:S(2)}, u32[]{:S(2)}) %collective-permute-start) | collective-permute-done | bytes 24608 | tf_op jit(solution)/shard_map/ppermute | solution.py:689
  15.7 0.0 copy-done.1
  15.7 0.0 copy-start.2
  15.7 0.6 copy-done.2
  16.3 1.9 %pack.1 = bf16[32,48,128]{2,1,0:T(8,128)(2,1)} custom-call(bf16[96,128]{1,0:T(8,128)(2,1)} %copy-done.2, bf16[96,128]{1,0:T(8,128)(2,1)} %split.1.own_ref, bf16[96,128]{1,0:T(8,128)(2,1)} %copy-done.1), custom_call_target="tpu_custom_call" | custom-call | tf_op jit(solution)/shard_map/pack/pallas_call | solution.py:691
  18.1 9.3 %all-to-all-start = ((bf16[32,48,128]{2,1,0:T(8,128)(2,1)}), bf16[32,48,128]{2,1,0:T(8,128)(2,1)S(1)}, u32[]{:S(2)}, u32[]{:S(2)}) async-start(bf16[32,48,128]{2,1,0:T(8,128)(2,1)} %pack.1), calls=%async_computation | async-start | bytes 786432 | tf_op jit(solution)/shard_map/all_to_all | solution.py:699
  27.5 1.4 %reshape.70.k1_ref = bf16[81,16]{1,0:T(8,128)(2,1)} reshape(bf16[3,3,3,3,16]{4,3,2,1,0:T(4,128)(2,1)} %bitcast.28) | data formatting | bytes 5184 | tf_op jit(solution)/shard_map/reshape | solution.py:622
  28.9 1.5 %reshape.72.k3_ref = bf16[162,16]{1,0:T(8,128)(2,1)} reshape(bf16[3,3,3,3,2,16]{5,4,3,2,1,0:T(2,128)(2,1)} %bitcast.27) | data formatting | bytes 10368 | tf_op jit(solution)/shard_map/reshape | solution.py:624
  30.3 4.4 %weights.1 = (bf16[384,128]{1,0:T(8,128)(2,1)}, bf16[768,128]{1,0:T(8,128)(2,1)}, bf16[4608,256]{1,0:T(8,128)(2,1)}, bf16[4608,256]{1,0:T(8,128)(2,1)}, bf16[115...) custom-call(bf16[81,16]{1,0:T(8,128)(2,1)} %reshape.70.k1_ref, bf16[1296,16]{1,0:T(8,128)(2,1)} %bitcast.26, ...), custom_call_target="tpu_custom_call" | custom-call | flops 1000000 | bytes 8000000 | tf_op jit(solution)/shard_map/weights/pallas_call | solution.py:592
  34.7 3.6 %all-to-all-done.in_ref = bf16[32,48,128]{2,1,0:T(8,128)(2,1)S(1)} async-done(((bf16[32,48,128]{2,1,0:T(8,128)(2,1)}), bf16[32,48,128]{2,1,0:T(8,128)(2,1)S(1)}, u32[]{:S(2)}, u32[]{:S(2)}) %all-to-all-start) | async-done | bytes 393248 | tf_op jit(solution)/shard_map/all_to_all | solution.py:699
  38.2 0.0 copy-start
  38.2 0.7 copy-done
  39.0 22.0 %flow.1 = (f32[32,8,128]{2,1,0:T(8,128)}, bf16[6,5,2,16,384]{4,3,2,1,0:T(8,128)(2,1)}, f32[3,32,128]{2,1,0:T(8,128)}) custom-call(bf16[32,48,128]{2,1,0:T(8,128)(2,1)} %copy-done, bf16[512,512]{1,0:T(8,128)(2,1)} %constant.6.clone.perm_hbm, bf16[384,128]{1,0:T(8,128)(2,1)} %get-tuple-element.26.w1_hbm, bf16[768,128]{1,0:T(8,128)(2,1)} %get-tuple-element.27.w3t_hbm, ...), custom_call_target="tpu_custom_call" | custom-call | flops 20000000000 | bytes 8000000 | tf_op jit(solution)/shard_map/flow/pallas_call | solution.py:632
  61.0 13.4 %all_to_all.20 = f32[32,8,128]{2,1,0:T(8,128)S(1)} all-to-all(f32[32,8,128]{2,1,0:T(8,128)} %get-tuple-element.32), channel_id=1, replica_groups=mesh['gx'=8,'gyh'=8,'gyl'=2,'gz'=2] {'gz','gx','gyl'}, dimensions={0} | all-to-all | bytes 262144 | tf_op jit(solution)/shard_map/all_to_all | solution.py:705
  74.4 0.6 broadcast_in_dim.4
  75.0 3.3 %all-to-all-start.2 = ((f32[8,8,128]{2,1,0:T(8,128)}), f32[8,8,128]{2,1,0:T(8,128)S(1)}, u32[]{:S(2)}, u32[]{:S(2)}) async-start(f32[8,8,128]{2,1,0:T(8,128)} %broadcast_in_dim.4), calls=%async_computation.2 | async-start | bytes 65536 | tf_op jit(solution)/shard_map/all_to_all | solution.py:724
  78.4 4.1 %input_grad.1 = f32[32,8,128]{2,1,0:T(8,128)} custom-call(bf16[6,5,2,16,384]{4,3,2,1,0:T(8,128)(2,1)} %get-tuple-element.33.cot1_hbm, f32[3,32,128]{2,1,0:T(8,128)} %get-tuple-element.34.held_ref, bf16[1152,128]{1,0:T(8,128)(2,1)} %get-tuple-element.35.w1t_hbm, bf16[512,512]{1,0:T(8,128)(2,1)} %constant.6.clone.perm_hbm), custom_call_target="tpu_custom_call" | custom-call | flops 500000000 | bytes 3000000 | tf_op jit(solution)/shard_map/input_grad/pallas_call | solution.py:706
  82.5 3.4 %all-to-all-done.2 = f32[8,8,128]{2,1,0:T(8,128)S(1)} async-done(((f32[8,8,128]{2,1,0:T(8,128)}), f32[8,8,128]{2,1,0:T(8,128)S(1)}, u32[]{:S(2)}, u32[]{:S(2)}) %all-to-all-start.2) | async-done | bytes 32800 | tf_op jit(solution)/shard_map/all_to_all | solution.py:724
  85.9 0.9 pad_maximum_fusion
  86.8 14.8 %all_to_all.21.in_ref = f32[32,16,128]{2,1,0:T(8,128)} all-to-all(f32[32,16,128]{2,1,0:T(8,128)S(1)} %pad_maximum_fusion), channel_id=1, replica_groups=mesh['gx'=8,'gyh'=8,'gyl'=2,'gz'=2] {'gz','gx','gyl'}, dimensions={0} | all-to-all | bytes 524288 | tf_op jit(solution)/shard_map/all_to_all | solution.py:727
  101.6 2.3 %unpack.1 = (f32[32,128]{1,0:T(8,128)}, f32[32,128]{1,0:T(8,128)}, f32[81,1,16]{2,1,0:T(1,128)}, f32[81,16,16]{2,1,0:T(8,128)}, f32[81,2,16]{2,1,0:T(2,128)}, /*...) custom-call(f32[32,16,128]{2,1,0:T(8,128)} %all_to_all.21.in_ref), custom_call_target="tpu_custom_call" | custom-call | tf_op jit(solution)/shard_map/unpack/pallas_call | solution.py:728
  (4 shorter events, 0.1 us)
Async XLA Ops:
  2.0 8.9 %collective-permute-start.1 = (bf16[96,128]{1,0:T(8,128)(2,1)}, bf16[96,128]{1,0:T(8,128)(2,1)S(1)}, u32[]{:S(2)}, u32[]{:S(2)}) collective-permute-start(bf16[96,128]{1,0:T(8,128)(2,1)} %split.1.own_ref), channel_id=1, source_target_pairs={{0,28},{4,0},{8,4},{12,8},{16,12},{20,16},{24,20},{28,24},{1,29},{... | collective-permute-start | bytes 73736 | tf_op jit(solution)/shard_map/ppermute | solution.py:690
  9.8 5.9 %collective-permute-start = (bf16[96,128]{1,0:T(8,128)(2,1)}, bf16[96,128]{1,0:T(8,128)(2,1)S(1)}, u32[]{:S(2)}, u32[]{:S(2)}) collective-permute-start(bf16[96,128]{1,0:T(8,128)(2,1)} %split.1.own_ref), channel_id=1, source_target_pairs={{0,4},{4,8},{8,12},{12,16},{16,20},{20,24},{24,28},{28,0},{1,5},{5... | collective-permute-start | bytes 73736 | tf_op jit(solution)/shard_map/ppermute | solution.py:689
  10.9 4.8 %copy-start.1 = (bf16[96,128]{1,0:T(8,128)(2,1)}, bf16[96,128]{1,0:T(8,128)(2,1)S(1)}, u32[]{:S(2)}) copy-start(bf16[96,128]{1,0:T(8,128)(2,1)S(1)} %collective-permute-done.1.high_ref) | copy-start | bytes 73732
  15.7 0.6 copy-start.2
  18.1 20.1 %all-to-all-start = ((bf16[32,48,128]{2,1,0:T(8,128)(2,1)}), bf16[32,48,128]{2,1,0:T(8,128)(2,1)S(1)}, u32[]{:S(2)}, u32[]{:S(2)}) async-start(bf16[32,48,128]{2,1,0:T(8,128)(2,1)} %pack.1), calls=%async_computation | async-start | bytes 786432 | tf_op jit(solution)/shard_map/all_to_all | solution.py:699
  38.2 0.7 copy-start
  75.0 10.8 %all-to-all-start.2 = ((f32[8,8,128]{2,1,0:T(8,128)}), f32[8,8,128]{2,1,0:T(8,128)S(1)}, u32[]{:S(2)}, u32[]{:S(2)}) async-start(f32[8,8,128]{2,1,0:T(8,128)} %broadcast_in_dim.4), calls=%async_computation.2 | async-start | bytes 65536 | tf_op jit(solution)/shard_map/all_to_all | solution.py:724

commit v2 on v1

--- a/solution.py
+++ b/solution.py
@@ -30,46 +30,27 @@
     return matrix
 
 
-def split_kernel(field_ref, mask_ref, out_ref):
+def pack_kernel(field_ref, mask_ref, out_ref, window):
     field = field_ref[...]
-    head = field.astype(BF16)
-    out_ref[0:32, :] = head
-    out_ref[32:64, :] = (field - head.astype(F32)).astype(BF16)
-    out_ref[64:96, :] = mask_ref[...].astype(F32).astype(BF16)
-
-
-def pack_kernel(low_ref, own_ref, high_ref, out_ref, window):
+    head = field.astype(BF16).astype(F32)
     empty = jnp.zeros((32, 128), F32)
-
-    def turn(ref):
-        both = ref[...].astype(F32)
-        near = jnp.concatenate([pltpu.roll(both, 7, 1), empty], axis=0).T
-        later = jnp.concatenate([empty, pltpu.roll(both, 119, 1)], axis=0).T
-        return near, later
-
-    low, low_later = turn(low_ref)
-    own, own_later = turn(own_ref)
-    high, high_later = turn(high_ref)
+    both = jnp.concatenate([head, field - head, mask_ref[...].astype(F32)], axis=0)
+    near = jnp.concatenate([pltpu.roll(both, 7, 1), empty], axis=0).T
+    later = jnp.concatenate([empty, pltpu.roll(both, 119, 1)], axis=0).T
     lane = lax.broadcasted_iota(jnp.int32, (128, 128), 1)
-    rows = [
-        jnp.where(lane < 96, low, pltpu.roll(own, 96, 1)),
-        jnp.where(lane < 64, pltpu.roll(own, 96, 1), pltpu.roll(high, 64, 1)),
-        pltpu.roll(high, 64, 1),
-        low_later,
-        pltpu.roll(own_later, 2, 0),
-        pltpu.roll(high_later, 4, 0),
-    ]
-    for number, value in enumerate(rows):
-        window[number, 0:128, :] = value
-        window[number, 128:144, :] = value[0:16, :]
-    lane = lax.broadcasted_iota(jnp.int32, (16, 128), 1)
+    rows = [near]
+    for kind in range(3):
+        turned = pltpu.roll(later, 64 - 32 * kind, 1)
+        rows.append(jnp.where(lane < 96, near, pltpu.roll(turned, 2 * kind, 0)))
+    for number in range(1, 4):
+        window[number - 1, 0:128, :] = rows[number]
+        window[number - 1, 128:144, :] = rows[number][0:16, :]
     row = lax.broadcasted_iota(jnp.int32, (16, 128), 0)
     for slot in range(32):
         here = slice(4 * slot, 4 * slot + 16)
-        out_ref[slot, 0:16, :] = window[0, here, :].astype(BF16)
-        out_ref[slot, 16:32, :] = window[1, here, :].astype(BF16)
-        tail = jnp.where(row < 2, window[3, here, :], jnp.where(row < 4, window[4, here, :], window[5, here, :]))
-        out_ref[slot, 32:48, :] = jnp.where(lane < 32, window[2, here, :], tail).astype(BF16)
+        out_ref[slot] = jnp.where(
+            row < 2, window[0, here, :], jnp.where(row < 4, window[1, here, :], window[2, here, :])
+        ).astype(BF16)
 
 
 def tile_dot(values):
@@ -226,22 +207,22 @@
 def pair_dot(ref, time, steps, pairs, w_ref):
     total = None
     for first in range(3):
-        for block in range(4):
-            rows = ref[pl.ds(time + first, steps), block // 2 : block // 2 + pairs, block % 2]
-            rows = rows.reshape(steps * pairs * 16, 384)
-            at = (first * 4 + block) * 384
-            term = jnp.dot(rows, w_ref[at : at + 384, :], preferred_element_type=F32)
+        for start in range(2):
+            sides = []
+            for block in (2 * start, 2 * start + 1):
+                rows = ref[pl.ds(time + first, steps), block // 2 : block // 2 + pairs, block % 2]
+                sides.append(rows.reshape(steps * pairs * 16, 384))
+            at = (first * 2 + start) * 768
+            term = jnp.dot(
+                jnp.concatenate(sides, axis=1), w_ref[at : at + 768, :], preferred_element_type=F32
+            )
             total = term if total is None else total + term
     return total
 
 
 def time_dot(ref, time, rows, w_ref):
-    total = None
-    for first in range(3):
-        block = ref[time + first].reshape(rows, 384)
-        term = jnp.dot(block, w_ref[first * 384 : first * 384 + 384, :], preferred_element_type=F32)
-        total = term if total is None else total + term
-    return total
+    sides = [ref[time + first].reshape(rows, ref.shape[-1]) for first in range(3)]
+    return jnp.dot(jnp.concatenate(sides, axis=1), w_ref[...], preferred_element_type=F32)
 
 
 def fold_group(values):
@@ -254,7 +235,7 @@
 
 
 def main_kernel(
-    in_ref, perm_hbm, w1_hbm, w3t_hbm, w2_hbm, w2t_hbm, w3_hbm, bias_hbm,
+    low_ref, own_ref, high_ref, perm_hbm, w1_hbm, w3t_hbm, w2_hbm, w2t_hbm, w3_hbm, bias_hbm,
     out_ref, cot1_hbm, held,
     gather, dense_f, dense_m, dense_z, frozen, frozen_x, act1, act2, pre0, pre1, flow, scale_c, shift_c,
     direct, third_x, cot2, cot1, perm_ref, w1_ref, w3t_ref, w2_ref, w2t_ref, w3_ref, bias_ref, sems,
@@ -278,17 +259,16 @@
         for step in range(count):
             body(step)
 
-    for source in range(32):
-        spot, half = source // 2, source % 2
-        lanes = slice(spot * 32, spot * 32 + 32)
-        tiles = [in_ref[source, 16 * tile : 16 * tile + 16, :].astype(F32) for tile in range(3)]
-        for block in range(3):
+    for block, ref in enumerate((own_ref, low_ref, high_ref)):
+        block = (1, 0, 2)[block]
+        for source in range(32):
+            spot, half = source // 2, source % 2
+            lanes = slice(spot * 32, spot * 32 + 32)
+            tile = ref[source].astype(F32)
             for kind in range(3):
-                piece = block * 3 + kind
-                at = piece % 4 * 32
-                gather[kind * 6 + block * 2 + half, 0:16, lanes] = tiles[piece // 4][:, at : at + 32]
-                at = 32 + 32 * kind
-                gather[kind * 6 + block * 2 + half, 16:18, lanes] = tiles[2][2 * block : 2 * block + 2, at : at + 32]
+                place = kind * 6 + block * 2 + half
+                gather[place, 0:16, lanes] = tile[:, 32 * kind : 32 * kind + 32]
+                gather[place, 16:18, lanes] = tile[2 * kind : 2 * kind + 2, 96:128]
     copies["perm"].wait()
     ordered = jnp.dot(
         gather[...].reshape(432, 512).astype(BF16), perm_ref[...], preferred_element_type=F32
@@ -316,12 +296,7 @@
     copies["bias"].wait()
 
     def first_layer(time):
-        total = bias_ref[0:1, :]
-        for first in range(3):
-            block = frozen_x[time + first].reshape(320, 128)
-            total = total + jnp.dot(
-                block, w1_ref[first * 128 : first * 128 + 128, :], preferred_element_type=F32
-            )
+        total = time_dot(frozen_x, time, 320, w1_ref) + bias_ref[0:1, :]
         for third, part in enumerate(shifted(jnp.tanh(total).reshape(20, 16, 128))):
             act1[time, :, :, :, third * 128 : third * 128 + 128] = part.reshape(10, 2, 16, 128)
 
@@ -330,13 +305,13 @@
     copies["w2"].wait()
 
     def second_layer(step):
-        total = pair_dot(act1, step * 2, 2, 9, w2_ref)
+        total = pair_dot(act1, step * 1, 1, 9, w2_ref)
         for member in range(2):
             values = jnp.tanh(total[:, member * 128 : member * 128 + 128] + bias_ref[1:2, :])
-            for third, part in enumerate(shifted(values.reshape(18, 16, 128))):
-                act2[pl.ds(step * 2, 2), :, member, :, third * 128 : third * 128 + 128] = part.reshape(2, 9, 16, 128)
-
-    repeat(7, second_layer)
+            for third, part in enumerate(shifted(values.reshape(9, 16, 128))):
+                act2[pl.ds(step * 1, 1), :, member, :, third * 128 : third * 128 + 128] = part.reshape(1, 9, 16, 128)
+
+    repeat(14, second_layer)
 
     copies["w3"].wait()
 
@@ -397,13 +372,7 @@
     copies["w3t"].wait()
 
     def second_cot(time):
-        total = None
-        for first in range(3):
-            block = third_x[time + first].reshape(192, 256)
-            term = jnp.dot(
-                block, w3t_ref[first * 256 : first * 256 + 256, :], preferred_element_type=F32
-            )
-            total = term if total is None else total + term
+        total = time_dot(third_x, time, 192, w3t_ref)
         act = act2[time + 3, :, :, :, 128:256].reshape(18, 16, 128)[3:15].astype(F32)
         values = total.reshape(12, 16, 128) * (1.0 - act * act)
         for third, part in enumerate(shifted(values)):
@@ -414,15 +383,15 @@
     copies["w2t"].wait()
 
     def first_cot(step):
-        total = pair_dot(cot2, step * 2, 2, 5, w2t_ref)
+        total = pair_dot(cot2, step * 3, 3, 5, w2t_ref)
         for member in range(2):
-            act = act1[pl.ds(step * 2 + 5, 2), 2 + member : 7 + member, 1 - member, :, 128:256]
-            act = act.astype(F32).reshape(10, 16, 128)
-            values = total[:, member * 128 : member * 128 + 128].reshape(10, 16, 128) * (1.0 - act * act)
+            act = act1[pl.ds(step * 3 + 5, 3), 2 + member : 7 + member, 1 - member, :, 128:256]
+            act = act.astype(F32).reshape(15, 16, 128)
+            values = total[:, member * 128 : member * 128 + 128].reshape(15, 16, 128) * (1.0 - act * act)
             for third, part in enumerate(shifted(values)):
-                cot1[pl.ds(step * 2, 2), :, member, :, third * 128 : third * 128 + 128] = part.reshape(2, 5, 16, 128)
-
-    repeat(3, first_cot)
+                cot1[pl.ds(step * 3, 3), :, member, :, third * 128 : third * 128 + 128] = part.reshape(3, 5, 16, 128)
+
+    repeat(2, first_cot)
 
     sent = pltpu.make_async_copy(cot1, cot1_hbm, sems.at[7])
     sent.start()
@@ -636,7 +605,7 @@
             shape((6, 5, 2, 16, 384), BF16),
             shape((3, 32, 128)),
         ],
-        in_specs=[VMEM_SPEC] + [HBM_SPEC] * 7,
+        in_specs=[VMEM_SPEC] * 3 + [HBM_SPEC] * 7,
         out_specs=[VMEM_SPEC, HBM_SPEC, VMEM_SPEC],
         scratch_shapes=[
             pltpu.VMEM((18, 24, 512), F32),
@@ -673,35 +642,28 @@
 
 def main_shapes():
     return [
-        shape((32, 48, 128), BF16), shape((512, 512), BF16), shape((384, 128), BF16), shape((768, 128), BF16),
+        shape((32, 16, 128), BF16), shape((32, 16, 128), BF16), shape((32, 16, 128), BF16), shape((512, 512), BF16), shape((384, 128), BF16), shape((768, 128), BF16),
         shape((4608, 256), BF16), shape((4608, 256), BF16), shape((1152, 128), BF16), shape((4, 128)),
     ]
 
 
 def local(field, parity_mask, kernel_one, bias_one, kernel_two, bias_two, kernel_three, bias_three):
-    own = pl.pallas_call(
-        split_kernel,
-        out_shape=shape((96, 128), BF16),
+    packed = pl.pallas_call(
+        pack_kernel,
+        out_shape=shape((32, 16, 128), BF16),
         in_specs=[VMEM_SPEC] * 2,
         out_specs=VMEM_SPEC,
-        name="split",
+        scratch_shapes=[pltpu.VMEM((3, 144, 128), F32)],
+        name="pack",
     )(field.reshape(32, 128), parity_mask.reshape(32, 128))
+    own = lax.all_to_all(packed, GROUP, 0, 0)
     low = lax.ppermute(own, "gyh", ring(8, 1))
     high = lax.ppermute(own, "gyh", ring(8, -1))
-    packed = pl.pallas_call(
-        pack_kernel,
-        out_shape=shape((32, 48, 128), BF16),
-        in_specs=[VMEM_SPEC] * 3,
-        out_specs=VMEM_SPEC,
-        scratch_shapes=[pltpu.VMEM((6, 144, 128), F32)],
-        name="pack",
-    )(low, own, high)
-    gathered = lax.all_to_all(packed, GROUP, 0, 0)
     w1, w3t, w2, w2t, w3, w1t, bias = run_weights(
         kernel_one, bias_one, kernel_two, bias_two, kernel_three, bias_three
     )
     perm = jnp.asarray(lane_permutation(), BF16)
-    shares, cot1, held = run_main(gathered, perm, w1, w3t, w2, w2t, w3, bias)
+    shares, cot1, held = run_main(low, own, high, perm, w1, w3t, w2, w2t, w3, bias)
     shares = lax.all_to_all(shares, GROUP, 0, 0)
     outputs = pl.pallas_call(
         input_grad_kernel,

time: 105 us -> 98.5 us (0.938)
  blocking collectives: 28.1 us -> 48.3 us
  starting transfers between devices: 20.5 us -> 8.49 us
  waiting for transfers between devices: 12.8 us -> 4.84 us
  Pallas kernels: 36 us -> 30.4 us
    all_to_all x0 -> x1, blocking collectives: none -> 18.5 us  [local(): own = lax.all_to_all(packed, GROUP, 0, 0)]
    all_to_all x1 -> x0, starting transfers between devices: 9.34 us -> none  [local(): gathered = lax.all_to_all(packed, GROUP, 0, 0)]
    pallas_call x1, Pallas kernels: 22 us -> 18 us  [run_main(): pl.pallas_call(main_kernel, out_shape=[shape((32, 8, 128)), shape((6, 5,...]
    all_to_all x1 -> x0, waiting for transfers between devices: 3.56 us -> none  [local(): gathered = lax.all_to_all(packed, GROUP, 0, 0)]
    ppermute x1, waiting for transfers between devices: 4.75 us -> 1.49 us  [local(): low = lax.ppermute(own, 'gyh', ring(8, 1))]
    ppermute x1, starting transfers between devices: 7.78 us -> 5.15 us  [local(): high = lax.ppermute(own, 'gyh', ring(8, -1))]
    all_to_all x1, blocking collectives: 13.4 us -> 15 us  [local(): shares = lax.all_to_all(shares, GROUP, 0, 0)]
    pallas_call x2 -> x1, Pallas kernels: 3.21 us -> 1.64 us  [local(): pl.pallas_call(pack_kernel, out_shape=shape((32, 16, 128), BF16), in_spec...]
  transfers between devices with their start and end apart: 4 -> 3, of which waited for: 4 -> 2; matrix products, arithmetic and copies ran while one was open for 3% -> 3% of each run, Pallas kernels for 8% -> 9%
where the time goes in v2:
time: 98.5 us; the launch traced here: 97.8 us
  blocking collectives  48.3 us (49%)
  Pallas kernels  30.4 us (31%)
  starting transfers between devices  8.49 us (9%)
  waiting for transfers between devices  4.84 us (5%)
  local copies, waits for them, and re-layouts  4.12 us (4%)
    all_to_all x1, blocking collectives, local(): own = lax.all_to_all(packed, GROUP, 0, 0)  18.5 us
    pallas_call x1, Pallas kernels, run_main(): pl.pallas_call(main_kernel, out_shape=[shape((32, 8, 128)), shape((6, 5,...  18 us
    all_to_all x1, blocking collectives, local(): shares = lax.all_to_all(shares, GROUP, 0, 0)  15 us
    all_to_all x1, blocking collectives, local(): last = lax.all_to_all(last, GROUP, 0, 0)  14.8 us
    ppermute x1, starting transfers between devices, local(): high = lax.ppermute(own, 'gyh', ring(8, -1))  5.15 us
    pallas_call x1, Pallas kernels, run_weights(): pl.pallas_call(weights_kernel, out_shape=[shape((384, 128), BF16), shape(...  4.41 us
    pallas_call x1, Pallas kernels, local(): pl.pallas_call(input_grad_kernel, out_shape=shape((32, 8, 128)), in_specs...  4.11 us
    all_to_all x1, waiting for transfers between devices, local(): share = lax.all_to_all(share, 'gyh', 0, 0)  3.35 us
  transfers between devices with their start and end apart: 3, of which 2 were waited for; matrix products, arithmetic and copies ran while one was open for 3% of the time, Pallas kernels for 9%

profile of v2, /device:TPU:1, one launch (start us, length us, event | category | flops | bytes accessed | tf_op | source)
XLA Modules:
  0.0 97.8 jit_solution(17539169582580306822)
XLA Ops:
  0.6 1.6 %pack.1 = bf16[32,16,128]{2,1,0:T(8,128)(2,1)} custom-call(f32[32,128]{1,0:T(8,128)} %bitcast.29, s32[32,128]{1,0:T(8,128)} %bitcast.30), custom_call_target="tpu_custom_call" | custom-call | tf_op jit(solution)/shard_map/pack/pallas_call | solution.py:651
  2.3 18.5 %all_to_all.20.own_ref = bf16[32,16,128]{2,1,0:T(8,128)(2,1)S(1)} all-to-all(bf16[32,16,128]{2,1,0:T(8,128)(2,1)} %pack.1), channel_id=1, replica_groups=mesh['gx'=8,'gyh'=8,'gyl'=2,'gz'=2] {'gz','gx','gyl'}, dimensions={0} | all-to-all | bytes 262144 | tf_op jit(solution)/shard_map/all_to_all | solution.py:659
  20.8 0.0 copy-start
  20.8 5.2 %collective-permute-start.1 = (bf16[32,16,128]{2,1,0:T(8,128)(2,1)S(1)}, bf16[32,16,128]{2,1,0:T(8,128)(2,1)S(1)}, u32[]{:S(2)}, u32[]{:S(2)}) collective-permute-start(bf16[32,16,128]{2,1,0:T(8,128)(2,1)S(1)} %all_to_all.20.own_ref), channel_id=1, source_target_pairs={{0,28},{4,0},{8,4},{12,8},{16,12},{20,16},{24,20},{28,24},{1,29},{... | collective-permute-start | bytes 393224 | tf_op jit(solution)/shard_map/ppermute | solution.py:661
  25.9 0.0 collective-permute-start
  25.9 1.4 %reshape.70.k1_ref = bf16[81,16]{1,0:T(8,128)(2,1)} reshape(bf16[3,3,3,3,16]{4,3,2,1,0:T(4,128)(2,1)} %bitcast.28) | data formatting | bytes 5184 | tf_op jit(solution)/shard_map/reshape | solution.py:591
  27.3 1.5 %reshape.72.k3_ref = bf16[162,16]{1,0:T(8,128)(2,1)} reshape(bf16[3,3,3,3,2,16]{5,4,3,2,1,0:T(2,128)(2,1)} %bitcast.27) | data formatting | bytes 10368 | tf_op jit(solution)/shard_map/reshape | solution.py:593
  28.8 4.4 %weights.1 = (bf16[384,128]{1,0:T(8,128)(2,1)}, bf16[768,128]{1,0:T(8,128)(2,1)}, bf16[4608,256]{1,0:T(8,128)(2,1)}, bf16[4608,256]{1,0:T(8,128)(2,1)}, bf16[115...) custom-call(bf16[81,16]{1,0:T(8,128)(2,1)} %reshape.70.k1_ref, bf16[1296,16]{1,0:T(8,128)(2,1)} %bitcast.26, ...), custom_call_target="tpu_custom_call" | custom-call | flops 1000000 | bytes 8000000 | tf_op jit(solution)/shard_map/weights/pallas_call | solution.py:561
  33.2 0.0 collective-permute-done.1.high_ref
  33.2 0.0 copy-start.1
  33.2 1.5 %collective-permute-done.low_ref = bf16[32,16,128]{2,1,0:T(8,128)(2,1)S(1)} collective-permute-done((bf16[32,16,128]{2,1,0:T(8,128)(2,1)S(1)}, bf16[32,16,128]{2,1,0:T(8,128)(2,1)S(1)}, u32[]{:S(2)}, u32[]{:S(2)}) %collective-permute-start) | collective-permute-done | bytes 131104 | tf_op jit(solution)/shard_map/ppermute | solution.py:660
  34.7 0.0 copy-start.2
  34.7 0.0 copy-done
  34.7 0.0 copy-done.1
  34.7 0.6 copy-done.2
  35.3 18.0 %flow.1 = (f32[32,8,128]{2,1,0:T(8,128)}, bf16[6,5,2,16,384]{4,3,2,1,0:T(8,128)(2,1)}, f32[3,32,128]{2,1,0:T(8,128)}) custom-call(bf16[32,16,128]{2,1,0:T(8,128)(2,1)} %copy-done.2, bf16[32,16,128]{2,1,0:T(8,128)(2,1)} %copy-done, bf16[32,16,128]{2,1,0:T(8,128)(2,1)} %copy-done.1, bf16[512,512]{1,0:T(8,128)(2,1)} %constant.6.clone.perm_hbm, ...), custom_call_target="tpu_custom_call" | custom-call | flops 20000000000 | bytes 8000000 | tf_op jit(solution)/shard_map/flow/pallas_call | solution.py:601
  53.3 15.0 %all_to_all.21 = f32[32,8,128]{2,1,0:T(8,128)S(1)} all-to-all(f32[32,8,128]{2,1,0:T(8,128)} %get-tuple-element.32), channel_id=1, replica_groups=mesh['gx'=8,'gyh'=8,'gyl'=2,'gz'=2] {'gz','gx','gyl'}, dimensions={0} | all-to-all | bytes 262144 | tf_op jit(solution)/shard_map/all_to_all | solution.py:667
  68.4 0.6 broadcast_in_dim.4
  69.0 3.3 %all-to-all-start.2 = ((f32[8,8,128]{2,1,0:T(8,128)}), f32[8,8,128]{2,1,0:T(8,128)S(1)}, u32[]{:S(2)}, u32[]{:S(2)}) async-start(f32[8,8,128]{2,1,0:T(8,128)} %broadcast_in_dim.4), calls=%async_computation.2 | async-start | bytes 65536 | tf_op jit(solution)/shard_map/all_to_all | solution.py:686
  72.3 4.1 %input_grad.1 = f32[32,8,128]{2,1,0:T(8,128)} custom-call(bf16[6,5,2,16,384]{4,3,2,1,0:T(8,128)(2,1)} %get-tuple-element.33.cot1_hbm, f32[3,32,128]{2,1,0:T(8,128)} %get-tuple-element.34.held_ref, bf16[1152,128]{1,0:T(8,128)(2,1)} %get-tuple-element.35.w1t_hbm, bf16[512,512]{1,0:T(8,128)(2,1)} %constant.6.clone.perm_hbm), custom_call_target="tpu_custom_call" | custom-call | flops 500000000 | bytes 3000000 | tf_op jit(solution)/shard_map/input_grad/pallas_call | solution.py:668
  76.4 3.3 %all-to-all-done.2 = f32[8,8,128]{2,1,0:T(8,128)S(1)} async-done(((f32[8,8,128]{2,1,0:T(8,128)}), f32[8,8,128]{2,1,0:T(8,128)S(1)}, u32[]{:S(2)}, u32[]{:S(2)}) %all-to-all-start.2) | async-done | bytes 32800 | tf_op jit(solution)/shard_map/all_to_all | solution.py:686
  79.8 0.9 pad_maximum_fusion
  80.7 14.8 %all_to_all.22.in_ref = f32[32,16,128]{2,1,0:T(8,128)} all-to-all(f32[32,16,128]{2,1,0:T(8,128)S(1)} %pad_maximum_fusion), channel_id=1, replica_groups=mesh['gx'=8,'gyh'=8,'gyl'=2,'gz'=2] {'gz','gx','gyl'}, dimensions={0} | all-to-all | bytes 524288 | tf_op jit(solution)/shard_map/all_to_all | solution.py:689
  95.5 2.3 %unpack.1 = (f32[32,128]{1,0:T(8,128)}, f32[32,128]{1,0:T(8,128)}, f32[81,1,16]{2,1,0:T(1,128)}, f32[81,16,16]{2,1,0:T(8,128)}, f32[81,2,16]{2,1,0:T(2,128)}, /*...) custom-call(f32[32,16,128]{2,1,0:T(8,128)} %all_to_all.22.in_ref), custom_call_target="tpu_custom_call" | custom-call | tf_op jit(solution)/shard_map/unpack/pallas_call | solution.py:690
  (4 shorter events, 0.1 us)
Async XLA Ops:
  20.8 13.9 %copy-start = (bf16[32,16,128]{2,1,0:T(8,128)(2,1)}, bf16[32,16,128]{2,1,0:T(8,128)(2,1)S(1)}, u32[]{:S(2)}) copy-start(bf16[32,16,128]{2,1,0:T(8,128)(2,1)S(1)} %all_to_all.20.own_ref) | copy-start | bytes 393220
  20.8 12.4 %collective-permute-start.1 = (bf16[32,16,128]{2,1,0:T(8,128)(2,1)S(1)}, bf16[32,16,128]{2,1,0:T(8,128)(2,1)S(1)}, u32[]{:S(2)}, u32[]{:S(2)}) collective-permute-start(bf16[32,16,128]{2,1,0:T(8,128)(2,1)S(1)} %all_to_all.20.own_ref), channel_id=1, source_target_pairs={{0,28},{4,0},{8,4},{12,8},{16,12},{20,16},{24,20},{28,24},{1,29},{... | collective-permute-start | bytes 393224 | tf_op jit(solution)/shard_map/ppermute | solution.py:661
  25.9 8.8 %collective-permute-start = (bf16[32,16,128]{2,1,0:T(8,128)(2,1)S(1)}, bf16[32,16,128]{2,1,0:T(8,128)(2,1)S(1)}, u32[]{:S(2)}, u32[]{:S(2)}) collective-permute-start(bf16[32,16,128]{2,1,0:T(8,128)(2,1)S(1)} %all_to_all.20.own_ref), channel_id=1, source_target_pairs={{0,4},{4,8},{8,12},{12,16},{16,20},{20,24},{24,28},{28,0},{1,5},{5... | collective-permute-start | bytes 393224 | tf_op jit(solution)/shard_map/ppermute | solution.py:660
  33.2 1.5 %copy-start.1 = (bf16[32,16,128]{2,1,0:T(8,128)(2,1)}, bf16[32,16,128]{2,1,0:T(8,128)(2,1)S(1)}, u32[]{:S(2)}) copy-start(bf16[32,16,128]{2,1,0:T(8,128)(2,1)S(1)} %collective-permute-done.1.high_ref) | copy-start | bytes 393220
  34.7 0.7 copy-start.2
  69.0 10.8 %all-to-all-start.2 = ((f32[8,8,128]{2,1,0:T(8,128)}), f32[8,8,128]{2,1,0:T(8,128)S(1)}, u32[]{:S(2)}, u32[]{:S(2)}) async-start(f32[8,8,128]{2,1,0:T(8,128)} %broadcast_in_dim.4), calls=%async_computation.2 | async-start | bytes 65536 | tf_op jit(solution)/shard_map/all_to_all | solution.py:686

commit v3 on v2

--- a/solution.py
+++ b/solution.py
@@ -2,7 +2,6 @@
 
 import jax
 import jax.numpy as jnp
-import numpy as np
 from jax import lax
 from jax.experimental import pallas as pl
 from jax.experimental.pallas import tpu as pltpu
@@ -13,21 +12,7 @@
 BF16 = jnp.bfloat16
 GROUP = ("gz", "gx", "gyl")
 VMEM_SPEC = pl.BlockSpec(memory_space=pltpu.VMEM)
-HBM_SPEC = pl.BlockSpec(memory_space=pltpu.HBM)
 VOLUME = 1048576.0
-
-
-def lane_permutation():
-    matrix = np.zeros((512, 512), np.float32)
-    for gz in range(2):
-        for gx in range(8):
-            for x in range(2):
-                for y in range(4):
-                    for z in range(4):
-                        source = (gz * 8 + gx) * 32 + x * 16 + y * 4 + z
-                        target = y * 128 + (gx * 2 + x) * 8 + gz * 4 + z
-                        matrix[source, target] = 1.0
-    return matrix
 
 
 def pack_kernel(field_ref, mask_ref, out_ref, window):
@@ -61,8 +46,7 @@
 
 def weights_kernel(
     k1_ref, k2_ref, k3_ref, b1_ref, b2_ref, b3_ref,
-    w1_hbm, w3t_hbm, w2_hbm, w2t_hbm, w3_hbm, w1t_hbm, bias_hbm,
-    w1_ref, w3t_ref, w2_ref, w2t_ref, w3_ref, w1t_ref, bias_ref, one, two, three, sems,
+    w1_ref, w3t_ref, w2_ref, w2t_ref, w3_ref, w1t_ref, bias_ref, perm_ref, one, two, three,
 ):
     def at(ex, ey, ez, et):
         return ((ex * 3 + ey) * 3 + ez) * 3 + et
@@ -136,22 +120,10 @@
     bias_ref[1:2, :] = jnp.concatenate([b2_ref[...]] * 8, axis=1)
     bias_ref[2:3, :] = jnp.broadcast_to(b3_ref[0:1, 0:1], (1, 128))
     bias_ref[3:4, :] = jnp.broadcast_to(b3_ref[0:1, 1:2], (1, 128))
-    copies = []
-    for number, (source, target) in enumerate(
-        (
-            (w1_ref, w1_hbm),
-            (w3t_ref, w3t_hbm),
-            (w2_ref, w2_hbm),
-            (w2t_ref, w2t_hbm),
-            (w3_ref, w3_hbm),
-            (w1t_ref, w1t_hbm),
-            (bias_ref, bias_hbm),
-        )
-    ):
-        copies.append(pltpu.make_async_copy(source, target, sems.at[number]))
-        copies[-1].start()
-    for copy in copies:
-        copy.wait()
+    lane = lax.broadcasted_iota(jnp.int32, (512, 512), 1)
+    source = (lane // 4 % 2 * 8 + lane // 16 % 8) * 32 + lane // 8 % 2 * 16 + lane // 128 * 4 + lane % 4
+    row = lax.broadcasted_iota(jnp.int32, (512, 512), 0)
+    perm_ref[...] = jnp.where(row == source, 1.0, 0.0).astype(BF16)
 
 
 def split_dot(values, matrix, parts, transposed=False):
@@ -235,26 +207,11 @@
 
 
 def main_kernel(
-    low_ref, own_ref, high_ref, perm_hbm, w1_hbm, w3t_hbm, w2_hbm, w2t_hbm, w3_hbm, bias_hbm,
-    out_ref, cot1_hbm, held,
+    low_ref, own_ref, high_ref, perm_ref, w1_ref, w3t_ref, w2_ref, w2t_ref, w3_ref, bias_ref,
+    out_ref, cot1, held,
     gather, dense_f, dense_m, dense_z, frozen, frozen_x, act1, act2, pre0, pre1, flow, scale_c, shift_c,
-    direct, third_x, cot2, cot1, perm_ref, w1_ref, w3t_ref, w2_ref, w2t_ref, w3_ref, bias_ref, sems,
+    direct, third_x, cot2,
 ):
-    copies = {}
-    for number, (name, source, target) in enumerate(
-        (
-            ("perm", perm_hbm, perm_ref),
-            ("w1", w1_hbm, w1_ref),
-            ("bias", bias_hbm, bias_ref),
-            ("w2", w2_hbm, w2_ref),
-            ("w3", w3_hbm, w3_ref),
-            ("w3t", w3t_hbm, w3t_ref),
-            ("w2t", w2t_hbm, w2t_ref),
-        )
-    ):
-        copies[name] = pltpu.make_async_copy(source, target, sems.at[number])
-        copies[name].start()
-
     def repeat(count, body):
         for step in range(count):
             body(step)
@@ -269,7 +226,6 @@
                 place = kind * 6 + block * 2 + half
                 gather[place, 0:16, lanes] = tile[:, 32 * kind : 32 * kind + 32]
                 gather[place, 16:18, lanes] = tile[2 * kind : 2 * kind + 2, 96:128]
-    copies["perm"].wait()
     ordered = jnp.dot(
         gather[...].reshape(432, 512).astype(BF16), perm_ref[...], preferred_element_type=F32
     )
@@ -292,8 +248,6 @@
 
     repeat(18, spread_frozen)
 
-    copies["w1"].wait()
-    copies["bias"].wait()
 
     def first_layer(time):
         total = time_dot(frozen_x, time, 320, w1_ref) + bias_ref[0:1, :]
@@ -302,7 +256,6 @@
 
     repeat(16, first_layer)
 
-    copies["w2"].wait()
 
     def second_layer(step):
         total = pair_dot(act1, step * 1, 1, 9, w2_ref)
@@ -313,7 +266,6 @@
 
     repeat(14, second_layer)
 
-    copies["w3"].wait()
 
     def third_layer(time):
         total = time_dot(act2, time, 288, w3_ref).reshape(18, 16, 128)
@@ -369,7 +321,6 @@
 
     repeat(10, spread_third)
 
-    copies["w3t"].wait()
 
     def second_cot(time):
         total = time_dot(third_x, time, 192, w3t_ref)
@@ -380,7 +331,6 @@
 
     repeat(8, second_cot)
 
-    copies["w2t"].wait()
 
     def first_cot(step):
         total = pair_dot(cot2, step * 3, 3, 5, w2t_ref)
@@ -393,8 +343,6 @@
 
     repeat(2, first_cot)
 
-    sent = pltpu.make_async_copy(cot1, cot1_hbm, sems.at[7])
-    sent.start()
     for time in range(4):
         rows = slice(time * 8, time * 8 + 8)
         held[0, rows, :] = flow[time + 4][4:12]
@@ -470,21 +418,9 @@
     for row, value in enumerate(sums):
         total = jnp.where(site == row, jnp.broadcast_to(value, (16, 128)), total)
     put(15, total)
-    sent.wait()
-
-
-def input_grad_kernel(
-    cot1_hbm, held_ref, w1t_hbm, perm_hbm, out_ref, own_out, rows_out, cot1_ref, w1t_ref, perm_ref, sems
-):
-    copies = [
-        pltpu.make_async_copy(cot1_hbm, cot1_ref, sems.at[0]),
-        pltpu.make_async_copy(w1t_hbm, w1t_ref, sems.at[1]),
-        pltpu.make_async_copy(perm_hbm, perm_ref, sems.at[2]),
-    ]
-    for copy in copies:
-        copy.start()
-    for copy in copies:
-        copy.wait()
+
+
+def input_grad_kernel(cot1_ref, held_ref, w1t_ref, perm_ref, out_ref, own_out, rows_out):
     for time in range(4):
         total = time_dot(cot1_ref, time, 160, w1t_ref).reshape(10, 16, 128)
         total = total[0:8] + pltpu.roll(total[1:9], 120, 2) + pltpu.roll(total[2:10], 112, 2)
@@ -568,23 +504,16 @@
             shape((1152, 128), BF16),
             shape((1152, 128), BF16),
             shape((4, 128)),
+            shape((512, 512), BF16),
         ],
         in_specs=[VMEM_SPEC] * 6,
-        out_specs=[HBM_SPEC] * 7,
+        out_specs=[VMEM_SPEC] * 8,
         scratch_shapes=[
-            pltpu.VMEM((384, 128), BF16),
-            pltpu.VMEM((768, 128), BF16),
-            pltpu.VMEM((4608, 256), BF16),
-            pltpu.VMEM((4608, 256), BF16),
-            pltpu.VMEM((1152, 128), BF16),
-            pltpu.VMEM((1152, 128), BF16),
-            pltpu.VMEM((4, 128), F32),
             pltpu.VMEM((81, 128), F32),
             pltpu.VMEM((1296, 128), F32),
             pltpu.VMEM((162, 128), F32),
-            pltpu.SemaphoreType.DMA((7,)),
         ],
-        compiler_params=pltpu.CompilerParams(vmem_limit_bytes=60 * 2**20),
+        compiler_params=pltpu.CompilerParams(vmem_limit_bytes=12 * 2**20),
         cost_estimate=pl.CostEstimate(flops=10**6, bytes_accessed=8 * 10**6, transcendentals=0),
         name="weights",
     )(
@@ -605,8 +534,8 @@
             shape((6, 5, 2, 16, 384), BF16),
             shape((3, 32, 128)),
         ],
-        in_specs=[VMEM_SPEC] * 3 + [HBM_SPEC] * 7,
-        out_specs=[VMEM_SPEC, HBM_SPEC, VMEM_SPEC],
+        in_specs=[VMEM_SPEC] * 10,
+        out_specs=[VMEM_SPEC] * 3,
         scratch_shapes=[
             pltpu.VMEM((18, 24, 512), F32),
             pltpu.VMEM((432, 128), F32),
@@ -624,17 +553,8 @@
             pltpu.VMEM((10, 14, 128), F32),
             pltpu.VMEM((10, 12, 16, 256), BF16),
             pltpu.VMEM((8, 6, 2, 16, 384), BF16),
-            pltpu.VMEM((6, 5, 2, 16, 384), BF16),
-            pltpu.VMEM((512, 512), BF16),
-            pltpu.VMEM((384, 128), BF16),
-            pltpu.VMEM((768, 128), BF16),
-            pltpu.VMEM((4608, 256), BF16),
-            pltpu.VMEM((4608, 256), BF16),
-            pltpu.VMEM((1152, 128), BF16),
-            pltpu.VMEM((4, 128), F32),
-            pltpu.SemaphoreType.DMA((8,)),
         ],
-        compiler_params=pltpu.CompilerParams(vmem_limit_bytes=60 * 2**20),
+        compiler_params=pltpu.CompilerParams(vmem_limit_bytes=28 * 2**20),
         cost_estimate=pl.CostEstimate(flops=2 * 10**10, bytes_accessed=8 * 10**6, transcendentals=10**6),
         name=name,
     )(*operands)
@@ -659,26 +579,21 @@
     own = lax.all_to_all(packed, GROUP, 0, 0)
     low = lax.ppermute(own, "gyh", ring(8, 1))
     high = lax.ppermute(own, "gyh", ring(8, -1))
-    w1, w3t, w2, w2t, w3, w1t, bias = run_weights(
+    w1, w3t, w2, w2t, w3, w1t, bias, perm = run_weights(
         kernel_one, bias_one, kernel_two, bias_two, kernel_three, bias_three
     )
-    perm = jnp.asarray(lane_permutation(), BF16)
     shares, cot1, held = run_main(low, own, high, perm, w1, w3t, w2, w2t, w3, bias)
     shares = lax.all_to_all(shares, GROUP, 0, 0)
     outputs = pl.pallas_call(
         input_grad_kernel,
         out_shape=shape((32, 8, 128)),
-        in_specs=[HBM_SPEC, VMEM_SPEC, HBM_SPEC, HBM_SPEC],
+        in_specs=[VMEM_SPEC] * 4,
         out_specs=VMEM_SPEC,
         scratch_shapes=[
             pltpu.VMEM((64, 128), F32),
             pltpu.VMEM((16, 512), F32),
-            pltpu.VMEM((6, 5, 2, 16, 384), BF16),
-            pltpu.VMEM((1152, 128), BF16),
-            pltpu.VMEM((512, 512), BF16),
-            pltpu.SemaphoreType.DMA((3,)),
         ],
-        compiler_params=pltpu.CompilerParams(vmem_limit_bytes=60 * 2**20),
+        compiler_params=pltpu.CompilerParams(vmem_limit_bytes=8 * 2**20),
         cost_estimate=pl.CostEstimate(flops=5 * 10**8, bytes_accessed=3 * 10**6, transcendentals=0),
         name="input_grad",
     )(cot1, held, w1t, perm)

time: 98.5 us -> 93.4 us (0.948)
  Pallas kernels: 30.4 us -> 21.1 us
  waiting for transfers between devices: 4.84 us -> 9.17 us
  local copies, waits for them, and re-layouts: 4.12 us -> 5.18 us
    pallas_call x1, Pallas kernels: 18 us -> 14.7 us  [run_main(): pl.pallas_call(main_kernel, out_shape=[shape((32, 8, 128)), shape((6, 5,...]
    pallas_call x1, Pallas kernels: 4.41 us -> 1.2 us  [run_weights(): pl.pallas_call(weights_kernel, out_shape=[shape((384, 128), BF16), shape(...]
    all_to_all x1, waiting for transfers between devices: 3.35 us -> 6.18 us  [local(): share = lax.all_to_all(share, 'gyh', 0, 0)]
    pallas_call x1, Pallas kernels: 4.11 us -> 1.27 us  [local(): pl.pallas_call(input_grad_kernel, out_shape=shape((32, 8, 128)), in_specs...]
    unnamed x6 -> x8, local copies, waits for them, and re-layouts: 0.65 us -> 2.93 us
    ppermute x1, waiting for transfers between devices: 1.49 us -> 2.98 us  [local(): low = lax.ppermute(own, 'gyh', ring(8, 1))]
  transfers between devices with their start and end apart: 3 -> 3, of which waited for: 2 -> 2; matrix products, arithmetic and copies ran while one was open for 3% -> 2% of each run, Pallas kernels for 9% -> 3%
where the time goes in v3:
time: 93.4 us; the launch traced here: 92.8 us
  blocking collectives  48.1 us (51%)
  Pallas kernels  21.1 us (23%)
  waiting for transfers between devices  9.17 us (10%)
  starting transfers between devices  8.49 us (9%)
  local copies, waits for them, and re-layouts  5.18 us (6%)
    all_to_all x1, blocking collectives, local(): own = lax.all_to_all(packed, GROUP, 0, 0)  18.5 us
    all_to_all x1, blocking collectives, local(): shares = lax.all_to_all(shares, GROUP, 0, 0)  14.8 us
    all_to_all x1, blocking collectives, local(): last = lax.all_to_all(last, GROUP, 0, 0)  14.8 us
    pallas_call x1, Pallas kernels, run_main(): pl.pallas_call(main_kernel, out_shape=[shape((32, 8, 128)), shape((6, 5,...  14.7 us
    all_to_all x1, waiting for transfers between devices, local(): share = lax.all_to_all(share, 'gyh', 0, 0)  6.18 us
    ppermute x1, starting transfers between devices, local(): high = lax.ppermute(own, 'gyh', ring(8, -1))  5.15 us
    all_to_all x1, starting transfers between devices, local(): share = lax.all_to_all(share, 'gyh', 0, 0)  3.34 us
    ppermute x1, waiting for transfers between devices, local(): low = lax.ppermute(own, 'gyh', ring(8, 1))  2.98 us
  transfers between devices with their start and end apart: 3, of which 2 were waited for; matrix products, arithmetic and copies ran while one was open for 2% of the time, Pallas kernels for 3%

profile of v3, /device:TPU:1, one launch (start us, length us, event | category | flops | bytes accessed | tf_op | source)
XLA Modules:
  0.0 92.8 jit_solution(8261461489034806621)
XLA Ops:
  0.6 1.6 %pack.1 = bf16[32,16,128]{2,1,0:T(8,128)(2,1)} custom-call(f32[32,128]{1,0:T(8,128)} %bitcast.32, s32[32,128]{1,0:T(8,128)} %bitcast.33), custom_call_target="tpu_custom_call" | custom-call | tf_op jit(solution)/shard_map/pack/pallas_call | solution.py:571
  2.3 18.5 %all_to_all.20.own_ref = bf16[32,16,128]{2,1,0:T(8,128)(2,1)S(1)} all-to-all(bf16[32,16,128]{2,1,0:T(8,128)(2,1)} %pack.1), channel_id=1, replica_groups=mesh['gx'=8,'gyh'=8,'gyl'=2,'gz'=2] {'gz','gx','gyl'}, dimensions={0} | all-to-all | bytes 262144 | tf_op jit(solution)/shard_map/all_to_all | solution.py:579
  20.8 5.2 %collective-permute-start.1 = (bf16[32,16,128]{2,1,0:T(8,128)(2,1)S(1)}, bf16[32,16,128]{2,1,0:T(8,128)(2,1)S(1)}, u32[]{:S(2)}, u32[]{:S(2)}) collective-permute-start(bf16[32,16,128]{2,1,0:T(8,128)(2,1)S(1)} %all_to_all.20.own_ref), channel_id=1, source_target_pairs={{0,28},{4,0},{8,4},{12,8},{16,12},{20,16},{24,20},{28,24},{1,29},{... | collective-permute-start | bytes 393224 | tf_op jit(solution)/shard_map/ppermute | solution.py:581
  25.9 0.0 collective-permute-start
  25.9 0.8 reshape.70.k1_ref
  26.7 0.8 reshape.72.k3_ref
  27.5 0.0 copy-start
  27.5 1.0 %copy-done = bf16[16,16,3,3,3,3]{1,0,5,4,3,2:T(8,128)(2,1)S(1)} copy-done((bf16[16,16,3,3,3,3]{1,0,5,4,3,2:T(8,128)(2,1)S(1)}, bf16[16,16,3,3,3,3]{1,0,5,4,3,2:T(8,128)(2,1)}, u32[]{:S(2)}) %copy-start) | copy-done | bytes 41496
  28.5 0.0 copy-start.1
  28.5 0.7 copy-done.1
  29.2 0.0 copy-start.2
  29.2 0.7 copy-done.2
  29.8 0.0 copy-start.3
  29.8 0.7 copy-done.3
  30.5 1.2 %weights.1 = (bf16[384,128]{1,0:T(8,128)(2,1)S(1)}, bf16[768,128]{1,0:T(8,128)(2,1)S(1)}, bf16[4608,256]{1,0:T(8,128)(2,1)S(1)}, bf16[4608,256]{1,0:T(8,128)(2,1...) custom-call(bf16[81,16]{1,0:T(8,128)(2,1)S(1)} %reshape.70.k1_ref, ...), custom_call_target="tpu_custom_call" | custom-call | flops 1000000 | bytes 8000000 | tf_op jit(solution)/shard_map/weights/pallas_call | solution.py:497
  31.7 0.0 collective-permute-done.1.high_ref
  31.7 3.0 %collective-permute-done.low_ref = bf16[32,16,128]{2,1,0:T(8,128)(2,1)S(1)} collective-permute-done((bf16[32,16,128]{2,1,0:T(8,128)(2,1)S(1)}, bf16[32,16,128]{2,1,0:T(8,128)(2,1)S(1)}, u32[]{:S(2)}, u32[]{:S(2)}) %collective-permute-start) | collective-permute-done | bytes 131104 | tf_op jit(solution)/shard_map/ppermute | solution.py:580
  34.7 14.7 %flow.1 = (f32[32,8,128]{2,1,0:T(8,128)S(1)}, bf16[6,5,2,16,384]{4,3,2,1,0:T(8,128)(2,1)S(1)}, f32[3,32,128]{2,1,0:T(8,128)S(1)}) custom-call(bf16[32,16,128]{2,1,0:T(8,128)(2,1)S(1)} %collective-permute-done.low_ref, bf16[32,16,128]{2,1,0:T(8,128)(2,1)S(1)} %all_to_all.20.own_ref, bf16[32,16,128]{2,1,0:T(8,128)(2,1)S(1)} %collective-permute-done.1.high_ref, ...), custom_call_target="tpu_custom_call" | custom-call | flops 20000000000 | bytes 8000000 | tf_op jit(solution)/shard_map/flow/pallas_call | solution.py:530
  49.4 14.8 %all_to_all.21 = f32[32,8,128]{2,1,0:T(8,128)S(1)} all-to-all(f32[32,8,128]{2,1,0:T(8,128)S(1)} %get-tuple-element.34), channel_id=1, replica_groups=mesh['gx'=8,'gyh'=8,'gyl'=2,'gz'=2] {'gz','gx','gyl'}, dimensions={0} | all-to-all | bytes 262144 | tf_op jit(solution)/shard_map/all_to_all | solution.py:586
  64.3 0.6 broadcast_in_dim.4
  64.9 3.3 %all-to-all-start.2 = ((f32[8,8,128]{2,1,0:T(8,128)}), f32[8,8,128]{2,1,0:T(8,128)S(1)}, u32[]{:S(2)}, u32[]{:S(2)}) async-start(f32[8,8,128]{2,1,0:T(8,128)} %broadcast_in_dim.4), calls=%async_computation.2 | async-start | bytes 65536 | tf_op jit(solution)/shard_map/all_to_all | solution.py:601
  68.2 1.3 %input_grad.1 = f32[32,8,128]{2,1,0:T(8,128)S(1)} custom-call(bf16[6,5,2,16,384]{4,3,2,1,0:T(8,128)(2,1)S(1)} %get-tuple-element.35.cot1_ref, f32[3,32,128]{2,1,0:T(8,128)S(1)} %get-tuple-element.36.held_ref, bf16[1152,128]{1,0:T(8,128)(2,1)S(1)} %get-tuple-element.37.w1t_ref, bf16[512,512]{1,0:T(8,128)(2,1)S(1)} %get-tuple-element.27.perm_ref), custom_call_target="tpu_custom_call" | custom-call | flops 500000000 | bytes 3000000 | tf_op jit(solution)/shard_map/input_grad/pallas_call | solution.py:587
  69.5 6.2 %all-to-all-done.2 = f32[8,8,128]{2,1,0:T(8,128)S(1)} async-done(((f32[8,8,128]{2,1,0:T(8,128)}), f32[8,8,128]{2,1,0:T(8,128)S(1)}, u32[]{:S(2)}, u32[]{:S(2)}) %all-to-all-start.2) | async-done | bytes 32800 | tf_op jit(solution)/shard_map/all_to_all | solution.py:601
  75.8 14.8 %all_to_all.22.in_ref = f32[32,16,128]{2,1,0:T(8,128)} all-to-all(f32[32,16,128]{2,1,0:T(8,128)S(1)} %pad_maximum_fusion), channel_id=1, replica_groups=mesh['gx'=8,'gyh'=8,'gyl'=2,'gz'=2] {'gz','gx','gyl'}, dimensions={0} | all-to-all | bytes 524288 | tf_op jit(solution)/shard_map/all_to_all | solution.py:604
  90.5 2.3 %unpack.1 = (f32[32,128]{1,0:T(8,128)}, f32[32,128]{1,0:T(8,128)}, f32[81,1,16]{2,1,0:T(1,128)}, f32[81,16,16]{2,1,0:T(8,128)}, f32[81,2,16]{2,1,0:T(2,128)}, /*...) custom-call(f32[32,16,128]{2,1,0:T(8,128)} %all_to_all.22.in_ref), custom_call_target="tpu_custom_call" | custom-call | tf_op jit(solution)/shard_map/unpack/pallas_call | solution.py:605
  (5 shorter events, 0.1 us)
Async XLA Ops:
  20.8 10.9 %collective-permute-start.1 = (bf16[32,16,128]{2,1,0:T(8,128)(2,1)S(1)}, bf16[32,16,128]{2,1,0:T(8,128)(2,1)S(1)}, u32[]{:S(2)}, u32[]{:S(2)}) collective-permute-start(bf16[32,16,128]{2,1,0:T(8,128)(2,1)S(1)} %all_to_all.20.own_ref), channel_id=1, source_target_pairs={{0,28},{4,0},{8,4},{12,8},{16,12},{20,16},{24,20},{28,24},{1,29},{... | collective-permute-start | bytes 393224 | tf_op jit(solution)/shard_map/ppermute | solution.py:581
  25.9 8.8 %collective-permute-start = (bf16[32,16,128]{2,1,0:T(8,128)(2,1)S(1)}, bf16[32,16,128]{2,1,0:T(8,128)(2,1)S(1)}, u32[]{:S(2)}, u32[]{:S(2)}) collective-permute-start(bf16[32,16,128]{2,1,0:T(8,128)(2,1)S(1)} %all_to_all.20.own_ref), channel_id=1, source_target_pairs={{0,4},{4,8},{8,12},{12,16},{16,20},{20,24},{24,28},{28,0},{1,5},{5... | collective-permute-start | bytes 393224 | tf_op jit(solution)/shard_map/ppermute | solution.py:580
  27.5 1.0 %copy-start = (bf16[16,16,3,3,3,3]{1,0,5,4,3,2:T(8,128)(2,1)S(1)}, bf16[16,16,3,3,3,3]{1,0,5,4,3,2:T(8,128)(2,1)}, u32[]{:S(2)}) copy-start(bf16[16,16,3,3,3,3]{1,0,5,4,3,2:T(8,128)(2,1)} %param.12) | copy-start | bytes 124420
  28.5 0.7 copy-start.1
  29.2 0.7 copy-start.2
  29.8 0.7 copy-start.3
  64.9 10.8 %all-to-all-start.2 = ((f32[8,8,128]{2,1,0:T(8,128)}), f32[8,8,128]{2,1,0:T(8,128)S(1)}, u32[]{:S(2)}, u32[]{:S(2)}) async-start(f32[8,8,128]{2,1,0:T(8,128)} %broadcast_in_dim.4), calls=%async_computation.2 | async-start | bytes 65536 | tf_op jit(solution)/shard_map/all_to_all | solution.py:601

commit v4 on v3

--- a/solution.py
+++ b/solution.py
@@ -51,9 +51,9 @@
     def at(ex, ey, ez, et):
         return ((ex * 3 + ey) * 3 + ez) * 3 + et
 
-    one[...] = tile_dot(k1_ref[...])
+    one[0:81, :] = tile_dot(k1_ref[...])
     two[...] = tile_dot(k2_ref[...])
-    three[...] = tile_dot(k3_ref[...])
+    three[0:162, :] = tile_dot(k3_ref[...])
     zone = lax.broadcasted_iota(jnp.int32, (8, 128), 1) // 16
     spot = lax.broadcasted_iota(jnp.int32, (8, 128), 0)
     wide = lax.broadcasted_iota(jnp.int32, (16, 128), 1) // 16
@@ -73,16 +73,18 @@
         return lambda off: slice(off * 2 + o, off * 2 + o + 1)
 
     for et in range(3):
-        w1_ref[et * 128 + 72 : et * 128 + 128, :] = jnp.zeros((56, 128), BF16)
+        block = []
         for ey in range(3):
-            block = [rows8(one, row_one, 2 - turned, ey, et, -1) for turned in range(3)]
-            w1_ref[et * 128 + ey * 24 : et * 128 + ey * 24 + 24, :] = jnp.concatenate(block, axis=0).astype(BF16)
+            block += [rows8(one, row_one, 2 - turned, ey, et, -1) for turned in range(3)]
+        block.append(jnp.zeros((56, 128), F32))
+        w1_ref[et * 128 : et * 128 + 128, :] = jnp.concatenate(block, axis=0).astype(BF16)
         for o in range(2):
             base = (et * 2 + o) * 128
-            w3t_ref[base + 72 : base + 128, :] = jnp.zeros((56, 128), BF16)
+            block = []
             for dy in range(3):
-                block = [rows8(three, row_three(o), turned, 2 - dy, 2 - et, 1) for turned in range(3)]
-                w3t_ref[base + dy * 24 : base + dy * 24 + 24, :] = jnp.concatenate(block, axis=0).astype(BF16)
+                block += [rows8(three, row_three(o), turned, 2 - dy, 2 - et, 1) for turned in range(3)]
+            block.append(jnp.zeros((56, 128), F32))
+            w3t_ref[base : base + 128, :] = jnp.concatenate(block, axis=0).astype(BF16)
         for ex in range(3):
             block = []
             for ey in range(3):
@@ -116,10 +118,16 @@
                 base = ((et * 4 + 3 * (1 - member)) * 3 + ex) * 128
                 w2_ref[base : base + 128, lanes] = zeros
                 w2t_ref[base : base + 128, lanes] = zeros
-    bias_ref[0:1, :] = jnp.concatenate([b1_ref[...]] * 8, axis=1)
-    bias_ref[1:2, :] = jnp.concatenate([b2_ref[...]] * 8, axis=1)
-    bias_ref[2:3, :] = jnp.broadcast_to(b3_ref[0:1, 0:1], (1, 128))
-    bias_ref[3:4, :] = jnp.broadcast_to(b3_ref[0:1, 1:2], (1, 128))
+    bias_ref[...] = jnp.concatenate(
+        [
+            jnp.concatenate([b1_ref[...]] * 8, axis=1),
+            jnp.concatenate([b2_ref[...]] * 8, axis=1),
+            jnp.broadcast_to(b3_ref[0:1, 0:1], (1, 128)),
+            jnp.broadcast_to(b3_ref[0:1, 1:2], (1, 128)),
+            jnp.zeros((4, 128), F32),
+        ],
+        axis=0,
+    )
     lane = lax.broadcasted_iota(jnp.int32, (512, 512), 1)
     source = (lane // 4 % 2 * 8 + lane // 16 % 8) * 32 + lane // 8 % 2 * 16 + lane // 128 * 4 + lane % 4
     row = lax.broadcasted_iota(jnp.int32, (512, 512), 0)
@@ -240,7 +248,7 @@
             dense_m[rows, :] = share[:, lanes]
             dense_z[rows, :] = head[:, lanes] * share[:, lanes]
     reverse = reverse_matrix()
-    frozen[...] = jnp.dot(dense_z[...].astype(BF16), reverse, preferred_element_type=F32)
+    frozen[...] = jnp.dot(dense_z[0:432, :].astype(BF16), reverse, preferred_element_type=F32)
 
     def spread_frozen(time):
         rows = slice(time * 24, time * 24 + 24)
@@ -305,7 +313,7 @@
             [active * (force * field * growth - 1.0) * (1.0 - scale * scale), empty], axis=0
         )
         shift_c[time] = jnp.concatenate([active * force, empty], axis=0)
-        direct[time] = force * (share + active * growth)
+        direct[time] = jnp.concatenate([force * (share + active * growth), empty], axis=0)
 
     repeat(10, force_step)
     scale_c[...] = jnp.dot(
@@ -434,7 +442,7 @@
                 rows_out[(kind * 2 + half) * 4 : (kind * 2 + half) * 4 + 4, y * 128 : y * 128 + 128] = own_out[
                     pl.ds(kind * 32 + half * 4 + y, 4, stride=8), :
                 ]
-    ordered = split_dot(rows_out[...], perm_ref[...], 3, transposed=True)
+    ordered = split_dot(rows_out[0:16, :], perm_ref[...], 3, transposed=True)
     for target in range(32):
         spot, half = target // 2, target % 2
         lanes = slice(spot * 32, spot * 32 + 32)
@@ -446,7 +454,7 @@
 def unpack_kernel(in_ref, flowed_ref, grad_ref, g1_ref, g2_ref, g3_ref, b1_ref, b2_ref, b3_ref, window, extra, turned_x):
     for source in range(32):
         window[4 * source : 4 * source + 4, :] = in_ref[source, 8:12, :]
-    turned = window[...].T
+    turned = window[0:128, :].T
     flowed_ref[...] = turned[0:32]
     grad_ref[...] = turned[32:64]
 
@@ -460,7 +468,7 @@
     for number in range(4):
         extra[number * 16 : number * 16 + 16, :] = group(11 + number)
     extra[64:128, :] = jnp.zeros((64, 128), F32)
-    turned_x[...] = extra[...].T
+    turned_x[0:128, :] = extra[...].T
     for et in range(3):
         lanes = slice(et * 16, et * 16 + 16)
         for ey in range(3):
@@ -503,15 +511,15 @@
             shape((4608, 256), BF16),
             shape((1152, 128), BF16),
             shape((1152, 128), BF16),
-            shape((4, 128)),
+            shape((8, 128)),
             shape((512, 512), BF16),
         ],
         in_specs=[VMEM_SPEC] * 6,
         out_specs=[VMEM_SPEC] * 8,
         scratch_shapes=[
-            pltpu.VMEM((81, 128), F32),
+            pltpu.VMEM((96, 128), F32),
             pltpu.VMEM((1296, 128), F32),
-            pltpu.VMEM((162, 128), F32),
+            pltpu.VMEM((176, 128), F32),
         ],
         compiler_params=pltpu.CompilerParams(vmem_limit_bytes=12 * 2**20),
         cost_estimate=pl.CostEstimate(flops=10**6, bytes_accessed=8 * 10**6, transcendentals=0),
@@ -538,9 +546,9 @@
         out_specs=[VMEM_SPEC] * 3,
         scratch_shapes=[
             pltpu.VMEM((18, 24, 512), F32),
-            pltpu.VMEM((432, 128), F32),
-            pltpu.VMEM((432, 128), F32),
-            pltpu.VMEM((432, 128), F32),
+            pltpu.VMEM((576, 128), F32),
+            pltpu.VMEM((576, 128), F32),
+            pltpu.VMEM((576, 128), F32),
             pltpu.VMEM((432, 128), F32),
             pltpu.VMEM((18, 20, 16, 128), BF16),
             pltpu.VMEM((16, 10, 2, 16, 384), BF16),
@@ -550,7 +558,7 @@
             pltpu.VMEM((12, 16, 128), F32),
             pltpu.VMEM((10, 16, 128), F32),
             pltpu.VMEM((10, 16, 128), F32),
-            pltpu.VMEM((10, 14, 128), F32),
+            pltpu.VMEM((10, 16, 128), F32),
             pltpu.VMEM((10, 12, 16, 256), BF16),
             pltpu.VMEM((8, 6, 2, 16, 384), BF16),
         ],
@@ -563,7 +571,7 @@
 def main_shapes():
     return [
         shape((32, 16, 128), BF16), shape((32, 16, 128), BF16), shape((32, 16, 128), BF16), shape((512, 512), BF16), shape((384, 128), BF16), shape((768, 128), BF16),
-        shape((4608, 256), BF16), shape((4608, 256), BF16), shape((1152, 128), BF16), shape((4, 128)),
+        shape((4608, 256), BF16), shape((4608, 256), BF16), shape((1152, 128), BF16), shape((8, 128)),
     ]
 
 
@@ -590,8 +598,8 @@
         in_specs=[VMEM_SPEC] * 4,
         out_specs=VMEM_SPEC,
         scratch_shapes=[
-            pltpu.VMEM((64, 128), F32),
-            pltpu.VMEM((16, 512), F32),
+            pltpu.VMEM((96, 128), F32),
+            pltpu.VMEM((24, 512), F32),
         ],
         compiler_params=pltpu.CompilerParams(vmem_limit_bytes=8 * 2**20),
         cost_estimate=pl.CostEstimate(flops=5 * 10**8, bytes_accessed=3 * 10**6, transcendentals=0),
@@ -610,7 +618,7 @@
         ],
         in_specs=[VMEM_SPEC],
         out_specs=[VMEM_SPEC] * 8,
-        scratch_shapes=[pltpu.VMEM((128, 128), F32), pltpu.VMEM((128, 128), F32), pltpu.VMEM((128, 128), F32)],
+        scratch_shapes=[pltpu.VMEM((136, 128), F32), pltpu.VMEM((128, 128), F32), pltpu.VMEM((136, 128), F32)],
         name="unpack",
     )(last)
     return (

time: 93.4 us -> 93.4 us (level)
  no operation moved by 1% of the time
where the time goes in v4:
time: 93.4 us; the launch traced here: 92.8 us
  blocking collectives  48.1 us (51%)
  Pallas kernels  21.1 us (23%)
  waiting for transfers between devices  9.22 us (10%)
  starting transfers between devices  8.49 us (9%)
  local copies, waits for them, and re-layouts  5.18 us (6%)
    all_to_all x1, blocking collectives, local(): own = lax.all_to_all(packed, GROUP, 0, 0)  18.5 us
    all_to_all x1, blocking collectives, local(): shares = lax.all_to_all(shares, GROUP, 0, 0)  14.8 us
    all_to_all x1, blocking collectives, local(): last = lax.all_to_all(last, GROUP, 0, 0)  14.8 us
    pallas_call x1, Pallas kernels, run_main(): pl.pallas_call(main_kernel, out_shape=[shape((32, 8, 128)), shape((6, 5,...  14.7 us
    all_to_all x1, waiting for transfers between devices, local(): share = lax.all_to_all(share, 'gyh', 0, 0)  6.18 us
    ppermute x1, starting transfers between devices, local(): high = lax.ppermute(own, 'gyh', ring(8, -1))  5.15 us
    all_to_all x1, starting transfers between devices, local(): share = lax.all_to_all(share, 'gyh', 0, 0)  3.34 us
    ppermute x1, waiting for transfers between devices, local(): low = lax.ppermute(own, 'gyh', ring(8, 1))  3.04 us
  transfers between devices with their start and end apart: 3, of which 2 were waited for; matrix products, arithmetic and copies ran while one was open for 2% of the time, Pallas kernels for 3%

profile of v4, /device:TPU:1, one launch (start us, length us, event | category | flops | bytes accessed | tf_op | source)
XLA Modules:
  0.0 92.8 jit_solution(4207659614147879231)
XLA Ops:
  0.6 1.6 %pack.1 = bf16[32,16,128]{2,1,0:T(8,128)(2,1)} custom-call(f32[32,128]{1,0:T(8,128)} %bitcast.32, s32[32,128]{1,0:T(8,128)} %bitcast.33), custom_call_target="tpu_custom_call" | custom-call | tf_op jit(solution)/shard_map/pack/pallas_call | solution.py:579
  2.3 18.5 %all_to_all.20.own_ref = bf16[32,16,128]{2,1,0:T(8,128)(2,1)S(1)} all-to-all(bf16[32,16,128]{2,1,0:T(8,128)(2,1)} %pack.1), channel_id=1, replica_groups=mesh['gx'=8,'gyh'=8,'gyl'=2,'gz'=2] {'gz','gx','gyl'}, dimensions={0} | all-to-all | bytes 262144 | tf_op jit(solution)/shard_map/all_to_all | solution.py:587
  20.8 5.2 %collective-permute-start.1 = (bf16[32,16,128]{2,1,0:T(8,128)(2,1)S(1)}, bf16[32,16,128]{2,1,0:T(8,128)(2,1)S(1)}, u32[]{:S(2)}, u32[]{:S(2)}) collective-permute-start(bf16[32,16,128]{2,1,0:T(8,128)(2,1)S(1)} %all_to_all.20.own_ref), channel_id=1, source_target_pairs={{0,28},{4,0},{8,4},{12,8},{16,12},{20,16},{24,20},{28,24},{1,29},{... | collective-permute-start | bytes 393224 | tf_op jit(solution)/shard_map/ppermute | solution.py:589
  25.9 0.0 collective-permute-start
  25.9 0.8 reshape.70.k1_ref
  26.7 0.8 reshape.72.k3_ref
  27.5 0.0 copy-start
  27.5 1.0 %copy-done = bf16[16,16,3,3,3,3]{1,0,5,4,3,2:T(8,128)(2,1)S(1)} copy-done((bf16[16,16,3,3,3,3]{1,0,5,4,3,2:T(8,128)(2,1)S(1)}, bf16[16,16,3,3,3,3]{1,0,5,4,3,2:T(8,128)(2,1)}, u32[]{:S(2)}) %copy-start) | copy-done | bytes 41496
  28.5 0.0 copy-start.1
  28.5 0.7 copy-done.1
  29.2 0.0 copy-start.2
  29.2 0.7 copy-done.2
  29.8 0.0 copy-start.3
  29.8 0.7 copy-done.3
  30.5 1.1 %weights.1 = (bf16[384,128]{1,0:T(8,128)(2,1)S(1)}, bf16[768,128]{1,0:T(8,128)(2,1)S(1)}, bf16[4608,256]{1,0:T(8,128)(2,1)S(1)}, bf16[4608,256]{1,0:T(8,128)(2,1...) custom-call(bf16[81,16]{1,0:T(8,128)(2,1)S(1)} %reshape.70.k1_ref, ...), custom_call_target="tpu_custom_call" | custom-call | flops 1000000 | bytes 8000000 | tf_op jit(solution)/shard_map/weights/pallas_call | solution.py:505
  31.6 0.0 collective-permute-done.1.high_ref
  31.6 3.0 %collective-permute-done.low_ref = bf16[32,16,128]{2,1,0:T(8,128)(2,1)S(1)} collective-permute-done((bf16[32,16,128]{2,1,0:T(8,128)(2,1)S(1)}, bf16[32,16,128]{2,1,0:T(8,128)(2,1)S(1)}, u32[]{:S(2)}, u32[]{:S(2)}) %collective-permute-start) | collective-permute-done | bytes 131104 | tf_op jit(solution)/shard_map/ppermute | solution.py:588
  34.7 14.7 %flow.1 = (f32[32,8,128]{2,1,0:T(8,128)S(1)}, bf16[6,5,2,16,384]{4,3,2,1,0:T(8,128)(2,1)S(1)}, f32[3,32,128]{2,1,0:T(8,128)S(1)}) custom-call(bf16[32,16,128]{2,1,0:T(8,128)(2,1)S(1)} %collective-permute-done.low_ref, bf16[32,16,128]{2,1,0:T(8,128)(2,1)S(1)} %all_to_all.20.own_ref, bf16[32,16,128]{2,1,0:T(8,128)(2,1)S(1)} %collective-permute-done.1.high_ref, ...), custom_call_target="tpu_custom_call" | custom-call | flops 20000000000 | bytes 8000000 | tf_op jit(solution)/shard_map/flow/pallas_call | solution.py:538
  49.4 14.8 %all_to_all.21 = f32[32,8,128]{2,1,0:T(8,128)S(1)} all-to-all(f32[32,8,128]{2,1,0:T(8,128)S(1)} %get-tuple-element.34), channel_id=1, replica_groups=mesh['gx'=8,'gyh'=8,'gyl'=2,'gz'=2] {'gz','gx','gyl'}, dimensions={0} | all-to-all | bytes 262144 | tf_op jit(solution)/shard_map/all_to_all | solution.py:594
  64.3 0.6 broadcast_in_dim.4
  64.9 3.3 %all-to-all-start.2 = ((f32[8,8,128]{2,1,0:T(8,128)}), f32[8,8,128]{2,1,0:T(8,128)S(1)}, u32[]{:S(2)}, u32[]{:S(2)}) async-start(f32[8,8,128]{2,1,0:T(8,128)} %broadcast_in_dim.4), calls=%async_computation.2 | async-start | bytes 65536 | tf_op jit(solution)/shard_map/all_to_all | solution.py:609
  68.2 1.3 %input_grad.1 = f32[32,8,128]{2,1,0:T(8,128)S(1)} custom-call(bf16[6,5,2,16,384]{4,3,2,1,0:T(8,128)(2,1)S(1)} %get-tuple-element.35.cot1_ref, f32[3,32,128]{2,1,0:T(8,128)S(1)} %get-tuple-element.36.held_ref, bf16[1152,128]{1,0:T(8,128)(2,1)S(1)} %get-tuple-element.37.w1t_ref, bf16[512,512]{1,0:T(8,128)(2,1)S(1)} %get-tuple-element.27.perm_ref), custom_call_target="tpu_custom_call" | custom-call | flops 500000000 | bytes 3000000 | tf_op jit(solution)/shard_map/input_grad/pallas_call | solution.py:595
  69.5 6.2 %all-to-all-done.2 = f32[8,8,128]{2,1,0:T(8,128)S(1)} async-done(((f32[8,8,128]{2,1,0:T(8,128)}), f32[8,8,128]{2,1,0:T(8,128)S(1)}, u32[]{:S(2)}, u32[]{:S(2)}) %all-to-all-start.2) | async-done | bytes 32800 | tf_op jit(solution)/shard_map/all_to_all | solution.py:609
  75.8 14.8 %all_to_all.22.in_ref = f32[32,16,128]{2,1,0:T(8,128)} all-to-all(f32[32,16,128]{2,1,0:T(8,128)S(1)} %pad_maximum_fusion), channel_id=1, replica_groups=mesh['gx'=8,'gyh'=8,'gyl'=2,'gz'=2] {'gz','gx','gyl'}, dimensions={0} | all-to-all | bytes 524288 | tf_op jit(solution)/shard_map/all_to_all | solution.py:612
  90.5 2.3 %unpack.1 = (f32[32,128]{1,0:T(8,128)}, f32[32,128]{1,0:T(8,128)}, f32[81,1,16]{2,1,0:T(1,128)}, f32[81,16,16]{2,1,0:T(8,128)}, f32[81,2,16]{2,1,0:T(2,128)}, /*...) custom-call(f32[32,16,128]{2,1,0:T(8,128)} %all_to_all.22.in_ref), custom_call_target="tpu_custom_call" | custom-call | tf_op jit(solution)/shard_map/unpack/pallas_call | solution.py:613
  (5 shorter events, 0.1 us)
Async XLA Ops:
  20.8 10.9 %collective-permute-start.1 = (bf16[32,16,128]{2,1,0:T(8,128)(2,1)S(1)}, bf16[32,16,128]{2,1,0:T(8,128)(2,1)S(1)}, u32[]{:S(2)}, u32[]{:S(2)}) collective-permute-start(bf16[32,16,128]{2,1,0:T(8,128)(2,1)S(1)} %all_to_all.20.own_ref), channel_id=1, source_target_pairs={{0,28},{4,0},{8,4},{12,8},{16,12},{20,16},{24,20},{28,24},{1,29},{... | collective-permute-start | bytes 393224 | tf_op jit(solution)/shard_map/ppermute | solution.py:589
  25.9 8.8 %collective-permute-start = (bf16[32,16,128]{2,1,0:T(8,128)(2,1)S(1)}, bf16[32,16,128]{2,1,0:T(8,128)(2,1)S(1)}, u32[]{:S(2)}, u32[]{:S(2)}) collective-permute-start(bf16[32,16,128]{2,1,0:T(8,128)(2,1)S(1)} %all_to_all.20.own_ref), channel_id=1, source_target_pairs={{0,4},{4,8},{8,12},{12,16},{16,20},{20,24},{24,28},{28,0},{1,5},{5... | collective-permute-start | bytes 393224 | tf_op jit(solution)/shard_map/ppermute | solution.py:588
  27.5 1.0 %copy-start = (bf16[16,16,3,3,3,3]{1,0,5,4,3,2:T(8,128)(2,1)S(1)}, bf16[16,16,3,3,3,3]{1,0,5,4,3,2:T(8,128)(2,1)}, u32[]{:S(2)}) copy-start(bf16[16,16,3,3,3,3]{1,0,5,4,3,2:T(8,128)(2,1)} %param.12) | copy-start | bytes 124420
  28.5 0.7 copy-start.1
  29.2 0.7 copy-start.2
  29.8 0.7 copy-start.3
  64.9 10.8 %all-to-all-start.2 = ((f32[8,8,128]{2,1,0:T(8,128)}), f32[8,8,128]{2,1,0:T(8,128)S(1)}, u32[]{:S(2)}, u32[]{:S(2)}) async-start(f32[8,8,128]{2,1,0:T(8,128)} %broadcast_in_dim.4), calls=%async_computation.2 | async-start | bytes 65536 | tf_op jit(solution)/shard_map/all_to_all | solution.py:609
